TPU v7x, 128 devices: a whole 4x4x4 slice. The times are simulated.
128 devices in a mesh: box: 128 (over x, y, z, core).
Axes of the slice: x: 4, y: 4, z: 4, core: 2. Of those that a mesh axis runs over, the one named last changes fastest.
Arguments:
- multipoles: bfloat16 [48, 49152], P(None, 'box'), may hold values from -6 to 6
- partners: int32 [189, 49152], P(None, 'box'), may hold values from 0 to 191, as said below
- partner_offset: int32 [189, 49152], P(None, 'box'), may hold values from 0 to 29, as said below
- classes: int32 [189, 49152], P(None, 'box'), may hold values from 0 to 315, as said below
- m2l_ops: bfloat16 [48, 15168], replicated, may hold values from -0.0625 to 0.0625
- m2m_ops: bfloat16 [48, 384], replicated, may hold values from -0.3125 to 0.3125
- coarse_ops: float32 [48, 48], replicated, may hold values from -0.875 to 0.875
- coupling: float32 [64, 64], replicated, may hold values from -0.75 to 0.75
- l2l_ops: float32 [48, 384], replicated, may hold values from -0.875 to 0.875
Outputs:
- locals_out: float32 [48, 49152], P(None, 'box')
- parents: float32 [48, 6144], P(None, 'box')
Inputs may be any that keep to these rules, and one draw needn't show every extreme that they name: `partners`: the source box s lies on the same device as the box, or among the first 48 or last 48 boxes of a device at most 7 devices away; every device has a source exactly 7 devices away. `partner_offset`: together with partners it names a box of the grid. classes[k, b] depends only on b mod 8 and k, and the 189 classes of one box are all different.
All inputs are finite; a program needn't handle non-finite values.
Results may differ from a plain program's by a relative error of at most 0.00035.
Values may be sent and summed in bfloat16 or wider, within the bound.
A program may use at most 128 MiB of HBM per device.

v0:
```python
import jax
import jax.numpy as jnp
from jax import lax
from jax.sharding import PartitionSpec as P

CLASSES = 316
REACH = 7
COARSE = 64


def passed_along(x, axis, by):
    size = lax.axis_size(axis)
    pairs = [(i, i + by) for i in range(size) if 0 <= i + by < size]
    return lax.ppermute(x, axis, pairs)


def octant_terms(table, chosen, classes_row, cube):
    rank = table.shape[0]
    slots, count = chosen.shape
    flat = chosen.reshape(slots * count)
    column_ids = jnp.arange(table.shape[1], dtype=jnp.int32)
    selector = (column_ids[:, None] == flat[None, :]).astype(jnp.bfloat16)
    gathered = jnp.dot(table, selector, preferred_element_type=jnp.float32).astype(jnp.bfloat16)
    stacked = gathered.reshape(rank * slots, count)
    picked = jnp.take(cube, classes_row, axis=1)
    operator = jnp.transpose(picked, (0, 2, 1)).reshape(rank, rank * slots)
    return jnp.dot(operator, stacked, preferred_element_type=jnp.float32)


def shards(
    multipoles, partners, partner_offset, classes, m2l_ops, m2m_ops, coarse_ops, coupling, l2l_ops
):
    rank, local_count = multipoles.shape
    device_count = lax.axis_size("box")
    device = lax.axis_index("box")
    rim_width = local_count // 8
    highest = lax.Precision.HIGHEST
    rims = jnp.concatenate(
        [multipoles[:, :rim_width], multipoles[:, local_count - rim_width :]], axis=1
    )
    sources = (2 * device - 2 * REACH + partner_offset) * (local_count // 2) + partners
    owner = sources // local_count
    within = sources % local_count
    distance = owner - device
    rim_index = jnp.where(within < rim_width, within, within - local_count + 2 * rim_width)
    received = []
    for amount in list(range(1, REACH + 1)) + list(range(-1, -REACH - 1, -1)):
        received.append(passed_along(rims, "box", amount))
    stacked = jnp.stack(received)
    table = jnp.concatenate(
        [multipoles, jnp.transpose(stacked, (1, 0, 2)).reshape(rank, -1)], axis=1
    )
    block_index = jnp.where(distance < 0, -distance - 1, distance + REACH - 1)
    remote = local_count + block_index * (2 * rim_width) + rim_index
    columns = jnp.where(distance == 0, within, remote)
    parent_count = local_count // 8
    children = jnp.transpose(multipoles.reshape(rank, parent_count, 8), (2, 0, 1)).reshape(
        8 * rank, parent_count
    )
    parents = jnp.dot(m2m_ops, children, preferred_element_type=jnp.float32)
    group = local_count * device_count // (8 * COARSE)
    parent_ids = device * parent_count + jnp.arange(parent_count, dtype=jnp.int32)
    member = (parent_ids[:, None] // group == jnp.arange(COARSE, dtype=jnp.int32)[None, :]).astype(
        jnp.float32
    )
    share = jnp.dot(parents, member, precision=highest) * jnp.float32(group ** (-0.5))
    coarse = lax.psum(share, "box")
    far = jnp.dot(jnp.dot(coarse_ops, coarse, precision=highest), coupling.T, precision=highest)
    cube = m2l_ops.reshape(rank, CLASSES, rank)
    outputs = []
    for octant in range(8):
        near = octant_terms(table, columns[:, octant::8], classes[:, octant], cube)
        lifted = jnp.dot(l2l_ops[:, octant * rank : (octant + 1) * rank], far, precision=highest)
        spread = jnp.dot(lifted, member.T, precision=highest)
        outputs.append(near + spread)
    locals_out = jnp.transpose(jnp.stack(outputs), (1, 2, 0)).reshape(rank, local_count)
    return (locals_out, parents)


def solution(mesh):
    placed = (
        P(None, "box"),
        P(None, "box"),
        P(None, "box"),
        P(None, "box"),
        P(),
        P(),
        P(),
        P(),
        P(),
    )
    return jax.shard_map(
        shards,
        mesh=mesh,
        in_specs=placed,
        out_specs=(P(None, "box"), P(None, "box")),
        check_vma=False,
    )
```

profile of v0, /device:TPU:3, one launch (start us, length us, event | category | flops | bytes accessed | tf_op | source)
XLA Modules:
  0.0 432.6 jit_solution(8308410450558645166)
XLA Ops:
  2.2 4.1 collective-permute-start
  6.4 3.5 collective-permute-start.1
  9.9 3.9 collective-permute-start.2
  13.8 2.6 collective-permute-start.3
  16.4 4.6 %collective-permute-start.4 = (bf16[48,96]{1,0:T(8,128)(2,1)}, bf16[48,96]{1,0:T(8,128)(2,1)S(1)}, u32[]{:S(2)}, u32[]{:S(2)}) collective-permute-start(bf16[48,96]{1,0:T(8,128)(2,1)} %pad_maximum_fusion), channel_id=1, source_target_pairs={{0,5},{1,6},{2,7},{3,8},{4,9},{5,10},{6,11},{7,12},{8,13},{9,14},{... | collective-permute-start | bytes 27656 | tf_op jit(solution)/shard_map/ppermute | solution.py:14
  21.0 2.1 slice_reduce_fusion
  24.5 64.6 %psum.7 = f32[48,64]{1,0:T(8,128)S(1)} all-reduce(f32[48,64]{1,0:T(8,128)S(1)} %convolution_multiply_fusion), channel_id=1, replica_groups=mesh['box'=128] {'box'}, use_global_device_ids=true, to_apply=%region_0.2 | all-reduce | flops 3072 | bytes 24576 | tf_op jit(solution)/shard_map/psum | solution.py:67
  104.0 5.6 %reshape.100 = bf16[48,316,48]{2,1,0:T(8,128)(2,1)} reshape(bf16[48,15168]{1,0:T(8,128)(2,1)S(1)} %copy-done.22) | data formatting | bytes 2912256 | tf_op jit(solution)/shard_map/reshape | solution.py:69
  109.6 6.5 %copy.11 = bf16[48,316,48]{2,0,1:T(8,128)(2,1)} copy(bf16[48,316,48]{2,1,0:T(8,128)(2,1)} %reshape.100) | data formatting | bytes 2912256 | tf_op jit(solution)/shard_map/reshape | solution.py:69
  116.1 4.4 %gather_fusion = bf16[189,48,48]{2,1,0:T(8,128)(2,1)} fusion(bf16[48,316,48]{2,0,1:T(8,128)(2,1)} %copy.11, s32[1024]{0:T(1024)S(1)} %pad_clamp_fusion.7), kind=kCustom, calls=%fused_computation.clone | custom fusion | bytes 1742580 | tf_op jit(solution)/shard_map/jit(_take)/gather | solution.py:25
  120.6 3.1 gather_fusion.1
  123.7 4.4 %gather_fusion.2 = bf16[189,48,48]{2,1,0:T(8,128)(2,1)} fusion(bf16[48,316,48]{2,0,1:T(8,128)(2,1)} %copy.11, s32[1024]{0:T(1024)S(1)} %pad_clamp_fusion.5), kind=kCustom, calls=%fused_computation.2.clone | custom fusion | bytes 1742580 | tf_op jit(solution)/shard_map/jit(_take)/gather | solution.py:25
  128.1 4.5 %gather_fusion.3 = bf16[189,48,48]{2,1,0:T(8,128)(2,1)} fusion(bf16[48,316,48]{2,0,1:T(8,128)(2,1)} %copy.11, s32[1024]{0:T(1024)S(1)} %pad_clamp_fusion.4), kind=kCustom, calls=%fused_computation.3.clone | custom fusion | bytes 1742580 | tf_op jit(solution)/shard_map/jit(_take)/gather | solution.py:25
  132.6 4.5 %gather_fusion.4 = bf16[189,48,48]{2,1,0:T(8,128)(2,1)} fusion(bf16[48,316,48]{2,0,1:T(8,128)(2,1)} %copy.11, s32[1024]{0:T(1024)S(1)} %pad_clamp_fusion.3), kind=kCustom, calls=%fused_computation.4.clone | custom fusion | bytes 1742580 | tf_op jit(solution)/shard_map/jit(_take)/gather | solution.py:25
  137.1 4.5 %gather_fusion.5 = bf16[189,48,48]{2,1,0:T(8,128)(2,1)} fusion(bf16[48,316,48]{2,0,1:T(8,128)(2,1)} %copy.11, s32[1024]{0:T(1024)S(1)} %pad_clamp_fusion.2), kind=kCustom, calls=%fused_computation.5.clone | custom fusion | bytes 1742580 | tf_op jit(solution)/shard_map/jit(_take)/gather | solution.py:25
  141.6 4.4 %gather_fusion.6 = bf16[189,48,48]{2,1,0:T(8,128)(2,1)} fusion(bf16[48,316,48]{2,0,1:T(8,128)(2,1)} %copy.11, s32[1024]{0:T(1024)S(1)} %pad_clamp_fusion.1), kind=kCustom, calls=%fused_computation.6.clone | custom fusion | bytes 1742580 | tf_op jit(solution)/shard_map/jit(_take)/gather | solution.py:25
  146.0 4.4 %gather_fusion.7 = bf16[189,48,48]{2,1,0:T(8,128)(2,1)} fusion(bf16[48,316,48]{2,0,1:T(8,128)(2,1)} %copy.11, s32[1024]{0:T(1024)S(1)} %pad_clamp_fusion), kind=kCustom, calls=%fused_computation.7.clone | custom fusion | bytes 1742580 | tf_op jit(solution)/shard_map/jit(_take)/gather | solution.py:25
  150.5 3.3 select_bitcast_fusion.7
  170.9 1.9 slice.81
  172.8 1.9 slice.84
  176.7 2.1 slice.90
  180.8 1.9 slice.96
  182.7 1.9 slice.99
  184.6 1.9 slice.102
  186.6 3.6 copy.12
  190.2 2.4 reshape.101
  193.5 3.6 copy.16
  197.1 2.3 reshape.106
  201.0 3.6 copy.18
  204.6 2.3 reshape.108
  208.5 4.0 copy.20
  212.5 2.3 reshape.110
  216.4 3.6 copy.22
  220.0 2.3 reshape.112
  223.9 3.6 copy.24
  227.5 2.4 reshape.114
  231.5 3.6 copy.26
  235.1 2.3 reshape.116
  239.0 2.1 copy.28
  241.1 2.3 reshape.118
  244.4 3.3 collective-permute-start.5
  248.4 3.1 collective-permute-start.6
  254.9 5.0 %collective-permute-start.8 = (bf16[48,96]{1,0:T(8,128)(2,1)}, bf16[48,96]{1,0:T(8,128)(2,1)S(1)}, u32[]{:S(2)}, u32[]{:S(2)}) collective-permute-start(bf16[48,96]{1,0:T(8,128)(2,1)} %pad_maximum_fusion), channel_id=1, source_target_pairs={{2,0},{3,1},{4,2},{5,3},{6,4},{7,5},{8,6},{9,7},{10,8},{11,9},{12,... | collective-permute-start | bytes 27656 | tf_op jit(solution)/shard_map/ppermute | solution.py:14
  260.7 4.6 %collective-permute-start.9 = (bf16[48,96]{1,0:T(8,128)(2,1)}, bf16[48,96]{1,0:T(8,128)(2,1)S(1)}, u32[]{:S(2)}, u32[]{:S(2)}) collective-permute-start(bf16[48,96]{1,0:T(8,128)(2,1)} %pad_maximum_fusion), channel_id=1, source_target_pairs={{3,0},{4,1},{5,2},{6,3},{7,4},{8,5},{9,6},{10,7},{11,8},{12,9},{13... | collective-permute-start | bytes 27656 | tf_op jit(solution)/shard_map/ppermute | solution.py:14
  265.3 3.7 collective-permute-start.10
  269.1 3.4 collective-permute-start.11
  274.5 2.7 collective-permute-start.13
  280.0 12.9 %fusion.23 = bf16[48,9072]{1,0:T(8,128)(2,1)S(1)} fusion(bf16[48,1728]{1,0:T(8,128)(2,1)S(1)} %constant_dynamic-update-slice_fusion.14, s32[9072]{0:T(1024)S(1)} %eq.140), kind=kOutput, calls=%fused_computation.39 | convolution fusion | flops 1521047808 | bytes 1073088 | tf_op jit(solution)/shard_map/dot_general | solution.py:23
  293.0 3.9 reshape.103
  296.8 12.7 %fusion.22 = bf16[48,9072]{1,0:T(8,128)(2,1)S(1)} fusion(bf16[48,1728]{1,0:T(8,128)(2,1)S(1)} %constant_dynamic-update-slice_fusion.14, s32[9072]{0:T(1024)S(1)} %copy-done.34), kind=kOutput, calls=%fused_computation.38 | convolution fusion | flops 1521047808 | bytes 1073088 | tf_op jit(solution)/shard_map/dot_general | solution.py:23
  309.6 3.0 reshape.107
  312.7 13.0 %fusion.21 = bf16[48,9072]{1,0:T(8,128)(2,1)S(1)} fusion(bf16[48,1728]{1,0:T(8,128)(2,1)S(1)} %copy-done.43, s32[9072]{0:T(1024)S(1)} %copy-done.35), kind=kOutput, calls=%fused_computation.37 | convolution fusion | flops 1521047808 | bytes 1073088 | tf_op jit(solution)/shard_map/dot_general | solution.py:23
  325.6 3.9 reshape.109
  329.6 12.7 %fusion.20 = bf16[48,9072]{1,0:T(8,128)(2,1)S(1)} fusion(bf16[48,1728]{1,0:T(8,128)(2,1)S(1)} %copy-done.43, s32[9072]{0:T(1024)S(1)} %copy-done.36), kind=kOutput, calls=%fused_computation.36 | convolution fusion | flops 1521047808 | bytes 1073088 | tf_op jit(solution)/shard_map/dot_general | solution.py:23
  342.4 3.9 reshape.111
  346.2 13.1 %fusion.19 = bf16[48,9072]{1,0:T(8,128)(2,1)S(1)} fusion(bf16[48,1728]{1,0:T(8,128)(2,1)S(1)} %copy-done.43, s32[9072]{0:T(1024)S(1)} %copy-done.37), kind=kOutput, calls=%fused_computation.35 | convolution fusion | flops 1521047808 | bytes 1073088 | tf_op jit(solution)/shard_map/dot_general | solution.py:23
  359.4 3.9 reshape.113
  363.3 12.7 %fusion.18 = bf16[48,9072]{1,0:T(8,128)(2,1)S(1)} fusion(bf16[48,1728]{1,0:T(8,128)(2,1)S(1)} %copy-done.43, s32[9072]{0:T(1024)S(1)} %copy-done.38), kind=kOutput, calls=%fused_computation.34 | convolution fusion | flops 1521047808 | bytes 1073088 | tf_op jit(solution)/shard_map/dot_general | solution.py:23
  376.1 3.9 reshape.115
  379.9 12.9 %fusion.17 = bf16[48,9072]{1,0:T(8,128)(2,1)S(1)} fusion(bf16[48,1728]{1,0:T(8,128)(2,1)S(1)} %copy-done.43, s32[9072]{0:T(1024)S(1)} %copy-done.39), kind=kOutput, calls=%fused_computation.33 | convolution fusion | flops 1521047808 | bytes 1073088 | tf_op jit(solution)/shard_map/dot_general | solution.py:23
  392.9 3.9 reshape.117
  396.8 13.5 %fusion.16 = bf16[48,9072]{1,0:T(8,128)(2,1)} fusion(bf16[48,1728]{1,0:T(8,128)(2,1)S(1)} %copy-done.43, s32[9072]{0:T(1024)S(1)} %eq.171), kind=kOutput, calls=%fused_computation.32 | convolution fusion | flops 1521047808 | bytes 1073088 | tf_op jit(solution)/shard_map/dot_general | solution.py:23
  410.2 5.2 %reshape.119 = bf16[9072,48]{1,0:T(8,128)(2,1)} reshape(bf16[48,9072]{1,0:T(8,128)(2,1)} %fusion.16) | data formatting | bytes 1741824 | tf_op jit(solution)/shard_map/reshape | solution.py:24
  415.5 2.3 fusion.70
  (190 shorter events, 74.3 us)
Async XLA Ops:
  0.6 23.5 %copy-start = (bf16[48,384]{1,0:T(8,128)(2,1)S(1)}, bf16[48,384]{1,0:T(8,128)(2,1)}, u32[]{:S(2)}) copy-start(bf16[48,384]{1,0:T(8,128)(2,1)} %param.16) | copy-start | bytes 110596
  0.6 103.4 %copy-start.22 = (bf16[48,15168]{1,0:T(8,128)(2,1)S(1)}, bf16[48,15168]{1,0:T(8,128)(2,1)}, u32[]{:S(2)}) copy-start(bf16[48,15168]{1,0:T(8,128)(2,1)} %param.15) | copy-start | bytes 4368388
  2.2 242.2 %collective-permute-start = (bf16[48,96]{1,0:T(8,128)(2,1)}, bf16[48,96]{1,0:T(8,128)(2,1)}, u32[]{:S(2)}, u32[]{:S(2)}) collective-permute-start(bf16[48,96]{1,0:T(8,128)(2,1)} %pad_maximum_fusion), channel_id=1, source_target_pairs={{0,1},{1,2},{2,3},{3,4},{4,5},{5,6},{6,7},{7,8},{8,9},{9,10},{10,1... | collective-permute-start | bytes 27656 | tf_op jit(solution)/shard_map/ppermute | solution.py:14
  6.4 242.1 %collective-permute-start.1 = (bf16[48,96]{1,0:T(8,128)(2,1)}, bf16[48,96]{1,0:T(8,128)(2,1)}, u32[]{:S(2)}, u32[]{:S(2)}) collective-permute-start(bf16[48,96]{1,0:T(8,128)(2,1)} %pad_maximum_fusion), channel_id=1, source_target_pairs={{0,2},{1,3},{2,4},{3,5},{4,6},{5,7},{6,8},{7,9},{8,10},{9,11},{10,... | collective-permute-start | bytes 27656 | tf_op jit(solution)/shard_map/ppermute | solution.py:14
  9.9 242.4 %collective-permute-start.2 = (bf16[48,96]{1,0:T(8,128)(2,1)}, bf16[48,96]{1,0:T(8,128)(2,1)}, u32[]{:S(2)}, u32[]{:S(2)}) collective-permute-start(bf16[48,96]{1,0:T(8,128)(2,1)} %pad_maximum_fusion), channel_id=1, source_target_pairs={{0,3},{1,4},{2,5},{3,6},{4,7},{5,8},{6,9},{7,10},{8,11},{9,12},{10... | collective-permute-start | bytes 27656 | tf_op jit(solution)/shard_map/ppermute | solution.py:14
  13.8 241.1 %collective-permute-start.3 = (bf16[48,96]{1,0:T(8,128)(2,1)}, bf16[48,96]{1,0:T(8,128)(2,1)}, u32[]{:S(2)}, u32[]{:S(2)}) collective-permute-start(bf16[48,96]{1,0:T(8,128)(2,1)} %pad_maximum_fusion), channel_id=1, source_target_pairs={{0,4},{1,5},{2,6},{3,7},{4,8},{5,9},{6,10},{7,11},{8,12},{9,13},{1... | collective-permute-start | bytes 27656 | tf_op jit(solution)/shard_map/ppermute | solution.py:14
  16.4 244.3 %collective-permute-start.4 = (bf16[48,96]{1,0:T(8,128)(2,1)}, bf16[48,96]{1,0:T(8,128)(2,1)S(1)}, u32[]{:S(2)}, u32[]{:S(2)}) collective-permute-start(bf16[48,96]{1,0:T(8,128)(2,1)} %pad_maximum_fusion), channel_id=1, source_target_pairs={{0,5},{1,6},{2,7},{3,8},{4,9},{5,10},{6,11},{7,12},{8,13},{9,14},{... | collective-permute-start | bytes 27656 | tf_op jit(solution)/shard_map/ppermute | solution.py:14
  24.3 85.3 %copy-start.40 = (f32[48,48]{1,0:T(8,128)}, f32[48,48]{1,0:T(8,128)S(1)}, u32[]{:S(2)}) copy-start(f32[48,48]{1,0:T(8,128)S(1)} %fusion.71) | copy-start | bytes 27652
  153.8 2.5 copy-start.2
  156.3 2.5 copy-start.3
  158.8 2.5 copy-start.4
  161.3 2.5 copy-start.5
  163.8 2.5 copy-start.6
  166.3 2.5 copy-start.7
  168.8 1.0 copy-start.23
  168.8 1.0 copy-start.24
  168.8 1.5 copy-start.25
  241.1 38.9 %copy-start.41 = (bf16[48,1728]{1,0:T(8,128)(2,1)S(1)}, bf16[48,1728]{1,0:T(8,128)(2,1)}, u32[]{:S(2)}) copy-start(bf16[48,1728]{1,0:T(8,128)(2,1)} %constant_dynamic-update-slice_fusion.15) | copy-start | bytes 497668
  244.4 20.9 %collective-permute-start.5 = (bf16[48,96]{1,0:T(8,128)(2,1)}, bf16[48,96]{1,0:T(8,128)(2,1)S(1)}, u32[]{:S(2)}, u32[]{:S(2)}) collective-permute-start(bf16[48,96]{1,0:T(8,128)(2,1)} %pad_maximum_fusion), channel_id=1, source_target_pairs={{0,6},{1,7},{2,8},{3,9},{4,10},{5,11},{6,12},{7,13},{8,14},{9,15},... | collective-permute-start | bytes 27656 | tf_op jit(solution)/shard_map/ppermute | solution.py:14
  248.4 20.6 %collective-permute-start.6 = (bf16[48,96]{1,0:T(8,128)(2,1)}, bf16[48,96]{1,0:T(8,128)(2,1)S(1)}, u32[]{:S(2)}, u32[]{:S(2)}) collective-permute-start(bf16[48,96]{1,0:T(8,128)(2,1)} %pad_maximum_fusion), channel_id=1, source_target_pairs={{0,7},{1,8},{2,9},{3,10},{4,11},{5,12},{6,13},{7,14},{8,15},{9,16}... | collective-permute-start | bytes 27656 | tf_op jit(solution)/shard_map/ppermute | solution.py:14
  252.3 20.2 %collective-permute-start.7 = (bf16[48,96]{1,0:T(8,128)(2,1)}, bf16[48,96]{1,0:T(8,128)(2,1)S(1)}, u32[]{:S(2)}, u32[]{:S(2)}) collective-permute-start(bf16[48,96]{1,0:T(8,128)(2,1)} %pad_maximum_fusion), channel_id=1, source_target_pairs={{1,0},{2,1},{3,2},{4,3},{5,4},{6,5},{7,6},{8,7},{9,8},{10,9},{11,1... | collective-permute-start | bytes 27656 | tf_op jit(solution)/shard_map/ppermute | solution.py:14
  254.9 19.6 %collective-permute-start.8 = (bf16[48,96]{1,0:T(8,128)(2,1)}, bf16[48,96]{1,0:T(8,128)(2,1)S(1)}, u32[]{:S(2)}, u32[]{:S(2)}) collective-permute-start(bf16[48,96]{1,0:T(8,128)(2,1)} %pad_maximum_fusion), channel_id=1, source_target_pairs={{2,0},{3,1},{4,2},{5,3},{6,4},{7,5},{8,6},{9,7},{10,8},{11,9},{12,... | collective-permute-start | bytes 27656 | tf_op jit(solution)/shard_map/ppermute | solution.py:14
  260.7 16.5 %collective-permute-start.9 = (bf16[48,96]{1,0:T(8,128)(2,1)}, bf16[48,96]{1,0:T(8,128)(2,1)S(1)}, u32[]{:S(2)}, u32[]{:S(2)}) collective-permute-start(bf16[48,96]{1,0:T(8,128)(2,1)} %pad_maximum_fusion), channel_id=1, source_target_pairs={{3,0},{4,1},{5,2},{6,3},{7,4},{8,5},{9,6},{10,7},{11,8},{12,9},{13... | collective-permute-start | bytes 27656 | tf_op jit(solution)/shard_map/ppermute | solution.py:14
  265.3 11.9 %collective-permute-start.10 = (bf16[48,96]{1,0:T(8,128)(2,1)}, bf16[48,96]{1,0:T(8,128)(2,1)S(1)}, u32[]{:S(2)}, u32[]{:S(2)}) collective-permute-start(bf16[48,96]{1,0:T(8,128)(2,1)} %pad_maximum_fusion), channel_id=1, source_target_pairs={{4,0},{5,1},{6,2},{7,3},{8,4},{9,5},{10,6},{11,7},{12,8},{13,9},{1... | collective-permute-start | bytes 27656 | tf_op jit(solution)/shard_map/ppermute | solution.py:14
  269.1 8.2 %collective-permute-start.11 = (bf16[48,96]{1,0:T(8,128)(2,1)}, bf16[48,96]{1,0:T(8,128)(2,1)S(1)}, u32[]{:S(2)}, u32[]{:S(2)}) collective-permute-start(bf16[48,96]{1,0:T(8,128)(2,1)} %pad_maximum_fusion), channel_id=1, source_target_pairs={{5,0},{6,1},{7,2},{8,3},{9,4},{10,5},{11,6},{12,7},{13,8},{14,9},{... | collective-permute-start | bytes 27656 | tf_op jit(solution)/shard_map/ppermute | solution.py:14
  272.5 5.9 %collective-permute-start.12 = (bf16[48,96]{1,0:T(8,128)(2,1)}, bf16[48,96]{1,0:T(8,128)(2,1)S(1)}, u32[]{:S(2)}, u32[]{:S(2)}) collective-permute-start(bf16[48,96]{1,0:T(8,128)(2,1)} %pad_maximum_fusion), channel_id=1, source_target_pairs={{6,0},{7,1},{8,2},{9,3},{10,4},{11,5},{12,6},{13,7},{14,8},{15,9},... | collective-permute-start | bytes 27656 | tf_op jit(solution)/shard_map/ppermute | solution.py:14
  274.5 5.2 %collective-permute-start.13 = (bf16[48,96]{1,0:T(8,128)(2,1)}, bf16[48,96]{1,0:T(8,128)(2,1)S(1)}, u32[]{:S(2)}, u32[]{:S(2)}) collective-permute-start(bf16[48,96]{1,0:T(8,128)(2,1)} %pad_maximum_fusion), channel_id=1, source_target_pairs={{7,0},{8,1},{9,2},{10,3},{11,4},{12,5},{13,6},{14,7},{15,8},{16,9}... | collective-permute-start | bytes 27656 | tf_op jit(solution)/shard_map/ppermute | solution.py:14
  280.0 16.8 %copy-start.42 = (bf16[48,1728]{1,0:T(8,128)(2,1)}, bf16[48,1728]{1,0:T(8,128)(2,1)S(1)}, u32[]{:S(2)}) copy-start(bf16[48,1728]{1,0:T(8,128)(2,1)S(1)} %constant_dynamic-update-slice_fusion.14) | copy-start | bytes 497668
  292.9 3.9 copy-start.34
  309.6 3.1 copy-start.35
  309.6 3.1 copy-start.43
  325.6 4.0 copy-start.36
  342.3 3.9 copy-start.37
  359.4 3.9 copy-start.38
  376.0 3.9 copy-start.39
  410.2 5.3 %copy-start.14 = (bf16[48,9072]{1,0:T(8,128)(2,1)S(1)}, bf16[48,9072]{1,0:T(8,128)(2,1)}, u32[]{:S(2)}) copy-start(bf16[48,9072]{1,0:T(8,128)(2,1)} %reshape.101) | copy-start | bytes 2612740
  415.5 2.3 copy-start.33
  415.5 2.5 copy-start.15
  417.8 1.7 copy-start.8
  417.8 1.9 copy-start.16
  419.7 1.7 copy-start.9
  419.7 1.9 copy-start.17
  421.5 1.7 copy-start.10
  421.5 1.9 copy-start.18
  423.4 1.7 copy-start.11
  423.4 1.9 copy-start.19
  425.2 1.7 copy-start.12
  425.2 1.9 copy-start.20
  427.1 1.7 copy-start.13
  427.1 1.9 copy-start.21
  427.1 5.2 %copy-start.1 = (bf16[48,384]{1,0:T(8,128)(2,1)S(1)}, bf16[48,384]{1,0:T(8,128)(2,1)}, u32[]{:S(2)}) copy-start(bf16[48,384]{1,0:T(8,128)(2,1)} %param.16) | copy-start | bytes 110596
  429.0 0.8 copy-start.26
  429.0 1.0 copy-start.29
  429.0 1.2 copy-start.27
  429.0 1.5 copy-start.31
  429.0 1.7 copy-start.28
  429.0 2.0 copy-start.32
  429.0 2.2 copy-start.30
where the time goes:
time: 441 us; the launch traced here: 433 us
  local copies, waits for them, and re-layouts  173 us (39%)
  matrix products  127 us (29%)
  blocking collectives  64.6 us (15%)
  starting transfers between devices  48.4 us (11%)
  other arithmetic  15.3 us (3%)
    dot_general x8, matrix products, octant_terms(): jnp.dot(table, selector, preferred_element_type=jnp.float32)  104 us
    psum x1, blocking collectives, shards(): coarse = lax.psum(share, 'box')  64.6 us
    ppermute x14, starting transfers between devices, passed_along(): return lax.ppermute(x, axis, pairs)  48.4 us
    gather x8, local copies, waits for them, and re-layouts, octant_terms(): picked = jnp.take(cube, classes_row, axis=1)  34.3 us
    reshape x8, local copies, waits for them, and re-layouts, octant_terms(): stacked = gathered.reshape(rank * slots, count)  31.7 us
    transpose x8, local copies, waits for them, and re-layouts, octant_terms(): operator = jnp.transpose(picked, (0, 2, 1)).reshape(rank, rank * slots)  27.5 us
    reshape x8, local copies, waits for them, and re-layouts, octant_terms(): operator = jnp.transpose(picked, (0, 2, 1)).reshape(rank, rank * slots)  18.7 us
    unnamed x104, local copies, waits for them, and re-layouts  18.3 us
  transfers between devices with their start and end apart: 14, of which 2 were waited for; matrix products, arithmetic and copies ran while one was open for 36% of the time, Pallas kernels for 0%

commit v1 on v0

v1 whole, which is shorter than its diff:
```python
import functools

import jax
import jax.numpy as jnp
from jax import lax
from jax.experimental import pallas as pl
from jax.experimental.pallas import tpu as pltpu
from jax.sharding import PartitionSpec as P

BF16 = jnp.bfloat16
F32 = jnp.float32
I32 = jnp.int32
MESH = pl.DeviceIdType.MESH
HIGHEST = lax.Precision.HIGHEST

DEVICES = 128
R = 48
K = 189
BOX = 384
CLASSES = 316
REACH = 7
RIM = 48
COARSE = 64
PARENTS = BOX // 8
GROUP = 96
BLOCKS = 2 * REACH
GROUPS = BLOCKS // 2
PAD_K = 192
CHUNKS = PAD_K // 4
FAR_ROWS = 64


def slot_of(distance):
    return distance + REACH if distance < 0 else distance + REACH - 1


DISTANCES = [s for a in range(1, REACH + 1) for s in (a, -a)]


def dot(a, b, precision=None):
    return jnp.dot(a, b, preferred_element_type=F32, precision=precision)


def dot_t(a, b, precision=None):
    return lax.dot_general(
        a, b, (((1,), (1,)), ((), ())), preferred_element_type=F32, precision=precision
    )


def iota(shape, dim):
    return lax.broadcasted_iota(I32, shape, dim)


def kernel(
    mult_hbm, part_hbm, off_hbm, cls_hbm, m2l_hbm, m2m_hbm, cops_hbm, coup_hbm, l2l_hbm,
    out_ref, par_ref,
    mult, part, off, cls, m2l, m2m, cops, coup, l2l,
    blk, rims, share, share_in, cbuf, lo_ref, hi_ref, strips, table, cube, gath, acc,
    in_sem, rim_send, rim_recv, pair_send, pair_recv, far_send, far_recv,
):
    me = lax.axis_index("box")
    chip = me // 2
    zc, yc, xc = chip % 4, (chip // 4) % 4, chip // 16
    core = me % 2

    loads = [
        pltpu.make_async_copy(src, dst, in_sem.at[i])
        for i, (src, dst) in enumerate(
            [
                (mult_hbm, mult), (m2m_hbm, m2m), (part_hbm, part), (off_hbm, off),
                (m2l_hbm, m2l), (cls_hbm.at[:, pl.ds(0, 128)], cls), (cops_hbm, cops),
                (coup_hbm, coup), (l2l_hbm, l2l),
            ]
        )
    ]
    for load in loads:
        load.start()

    def chip_peer(z, y, x):
        return ((x * 4 + y) * 4 + z) * 2 + core

    z_peers = [chip_peer((zc + m) % 4, yc, xc) for m in (1, 2, 3)]
    y_peers = [chip_peer(zc, (yc + m) % 4, xc) for m in (1, 2, 3)]
    x_peers = [chip_peer(zc, yc, (xc + m) % 4) for m in (1, 2, 3)]
    partner = me + 1 - 2 * core

    def valid(distance):
        return me + distance < DEVICES if distance > 0 else me + distance >= 0

    barrier = pltpu.get_barrier_semaphore()
    for distance in DISTANCES:
        @pl.when(valid(distance))
        def _():
            pl.semaphore_signal(
                barrier, inc=1, device_id=(me + distance,), device_id_type=MESH
            )
    for peer in y_peers + x_peers:
        pl.semaphore_signal(barrier, inc=1, device_id=(peer,), device_id_type=MESH)

    loads[0].wait()
    own = mult[...]
    own32 = own.astype(F32)
    lane = iota((R, 128), 1)
    upper = pltpu.roll(own32[:, 256:384], 96, 1)
    blk[...] = jnp.where(
        lane < RIM, own32[:, 0:128], jnp.where(lane < 2 * RIM, upper, 0.0)
    ).astype(BF16)

    expected = jnp.minimum(me, REACH) + jnp.minimum(DEVICES - 1 - me, REACH) + 6
    pl.semaphore_wait(barrier, expected)

    def rim_copy(distance):
        slot = slot_of(-distance)
        return pltpu.make_async_remote_copy(
            src_ref=blk,
            dst_ref=rims.at[slot],
            send_sem=rim_send.at[slot],
            recv_sem=rim_recv.at[slot],
            device_id=(me + distance,),
            device_id_type=MESH,
        )

    for distance in DISTANCES:
        @pl.when(valid(distance))
        def _():
            rim_copy(distance).start()

        @pl.when(jnp.logical_not(valid(distance)))
        def _():
            rims[slot_of(distance)] = jnp.zeros((R, 128), BF16)

    loads[1].wait()
    stacked = jnp.concatenate([m2m[:, R * j:R * j + R] for j in range(8)], axis=0)
    shifted = dot(stacked, own)
    octant = iota((R, BOX), 1) % 8
    mixed = jnp.zeros((R, BOX), F32)
    for j in range(8):
        mixed = jnp.where(octant == j, shifted[R * j:R * j + R], mixed)
    pool = (iota((BOX, PARENTS), 0) // 8 == iota((BOX, PARENTS), 1)).astype(F32)
    parents = dot(mixed, pool, HIGHEST)
    par_ref[...] = parents
    ones = jnp.ones((8, PARENTS), F32)
    total = dot_t(ones, parents, HIGHEST) * jnp.float32(GROUP ** (-0.5))
    share[...] = jnp.zeros((1, 128), F32)
    share[:, 0:R] = total[0:1, :]
    pair = pltpu.make_async_remote_copy(
        src_ref=share, dst_ref=share_in, send_sem=pair_send, recv_sem=pair_recv,
        device_id=(partner,), device_id_type=MESH,
    )
    pair.start()

    for i in range(BLOCKS):
        if i < BOX // 32:
            piece = own32[:, 128 * (i // 4):128 * (i // 4) + 128]
            shift = (96 - 32 * (i % 4)) % 128
            if shift:
                piece = pltpu.roll(piece, shift, 1)
            strips[i] = jnp.where(lane >= 2 * RIM, piece, 0.0).astype(BF16)
        else:
            strips[i] = jnp.zeros((R, 128), BF16)

    loads[2].wait()
    loads[3].wait()
    lo_ref[...] = jnp.zeros((PAD_K, BOX), F32)
    hi_ref[...] = jnp.full((PAD_K, BOX), GROUPS, I32)
    within, half = part[...], off[...]
    second = half & 1
    pos = half >> 1
    here = pos == REACH
    local = within + 192 * second
    local_col = ((local >> 5) << 7) + 96 + (local & 31)
    block = jnp.where(pos > REACH, pos - 1, pos)
    remote_col = (block << 7) + within + second * (RIM - 144)
    col = jnp.where(here, local_col, remote_col)
    lo_ref[0:K, :] = (col & 255).astype(F32)
    hi_ref[0:K, :] = col >> 8

    loads[4].wait()
    row, column = iota((256, 512), 0), iota((256, 512), 1)
    inner = column & 63
    start = R * (column >> 7)
    live = inner < R
    first = jnp.where(live & (row == start + inner), 1.0, 0.0).astype(BF16)
    second_half = jnp.where(live & (row == start + 64 + inner), 1.0, 0.0).astype(BF16)

    def spread(step, _):
        tops, bottoms = [], []
        for u in range(3):
            base = pl.multiple_of((step * 3 + u) * 384, 128)
            tops.append(m2l[:, pl.ds(base, 256)])
            bottoms.append(m2l[:, pl.ds(pl.multiple_of(base + 128, 128), 256)])
        a = dot(jnp.concatenate(tops, axis=0), first).astype(BF16)
        b = dot(jnp.concatenate(bottoms, axis=0), second_half).astype(BF16)
        for u in range(3):
            for j in range(4):
                cube[(step * 3 + u) * 8 + j] = a[R * u:R * u + R, 128 * j:128 * j + 128]
                cube[(step * 3 + u) * 8 + 4 + j] = b[R * u:R * u + R, 128 * j:128 * j + 128]
        return 0

    lax.fori_loop(0, 13, spread, 0)
    tail = dot(m2l[:, 39 * 384:CLASSES * R], first[0:192, :]).astype(BF16)
    for j in range(4):
        cube[312 + j] = tail[:, 128 * j:128 * j + 128]

    def clear(step, _):
        for q in range(4):
            at = pl.multiple_of(step * 256 + 64 * q + R, 16)
            gath[pl.ds(at, 16), :] = jnp.zeros((16, BOX), BF16)
        return 0

    lax.fori_loop(0, CHUNKS, clear, 0)

    pair.wait()
    cbuf[chip] = share[...] + share_in[...]

    def far_copies(stage, peers, start, count):
        return [
            pltpu.make_async_remote_copy(
                src_ref=cbuf.at[pl.ds(start, count)],
                dst_ref=cbuf.at[pl.ds(start, count)],
                send_sem=far_send.at[stage, m],
                recv_sem=far_recv.at[stage, m],
                device_id=(peer,),
                device_id_type=MESH,
            )
            for m, peer in enumerate(peers)
        ]

    along_z = far_copies(0, z_peers, chip, 1)
    along_y = far_copies(1, y_peers, (chip // 4) * 4, 4)
    along_x = far_copies(2, x_peers, (chip // 16) * 16, 16)
    for copy in along_z:
        copy.start()

    for distance in DISTANCES:
        @pl.when(valid(distance))
        def _():
            rim_copy(-distance).wait_recv()
    for i in range(BLOCKS):
        g, side = i // 2, i % 2
        table[R * g:R * g + R, 128 * side:128 * side + 128] = jnp.where(
            lane < 2 * RIM, rims[i].astype(F32), strips[i].astype(F32)
        ).astype(BF16)

    index = iota((256, 128), 0).astype(F32).astype(BF16)

    def one_hot(lo, k):
        pieces = []
        for j in range(3):
            wanted = jnp.broadcast_to(lo[k:k + 1, 128 * j:128 * j + 128], (256, 128))
            pieces.append(
                jnp.where(wanted.astype(BF16) == index, jnp.ones((), BF16), jnp.zeros((), BF16))
            )
        return jnp.concatenate(pieces, axis=1)

    def gather(step, _):
        base = pl.multiple_of(step * 16, 16)
        lo = lo_ref[pl.ds(base, 16), :]
        hi = hi_ref[pl.ds(base, 16), :]
        for p in range(0, 16, 2):
            hot = jnp.concatenate([one_hot(lo, p), one_hot(lo, p + 1)], axis=1)
            found = dot(table[...], hot)
            for q in range(2):
                wanted = jnp.broadcast_to(hi[p + q:p + q + 1, :], (R, BOX))
                value = jnp.zeros((R, BOX), F32)
                for g in range(GROUPS):
                    part_of = found[R * g:R * g + R, BOX * q:BOX * q + BOX]
                    value = jnp.where(wanted == g, part_of, value)
                at = pl.multiple_of(step * 1024 + 64 * (p + q), 64)
                gath[pl.ds(at, R), :] = value.astype(BF16)
        return 0

    lax.fori_loop(0, 4, gather, 0)
    for copy in along_z:
        copy.wait()
    for copy in along_y:
        copy.start()
    lax.fori_loop(4, 8, gather, 0)
    for copy in along_y:
        copy.wait()
    for copy in along_x:
        copy.start()
    lax.fori_loop(8, 12, gather, 0)
    for copy in along_x:
        copy.wait()

    for load in loads[6:9]:
        load.wait()
    coarse = cbuf[...].reshape(COARSE, 128)
    mixed_far = dot(coup[...], coarse, HIGHEST)
    mine = jnp.sum(
        jnp.where(iota((COARSE, 128), 0) == chip, mixed_far, 0.0), axis=0, keepdims=True
    )
    far = dot_t(jnp.broadcast_to(mine[:, 0:R], (8, R)), cops[...], HIGHEST)
    tile = (iota((R, BOX), 1) % R == iota((R, BOX), 0)).astype(F32)
    far_tiled = dot(far, tile, HIGHEST)
    terms = l2l[...] * far_tiled[0:1, :]
    by_octant = (iota((BOX, BOX), 0) // R == iota((BOX, BOX), 1) % 8).astype(F32)
    lifted = dot(terms, by_octant, HIGHEST)

    loads[5].wait()
    acc[...] = jnp.zeros(acc.shape, F32)
    lower = iota((R, 128), 1).astype(F32).astype(BF16) < jnp.full((), 64, BF16)

    def translate(step, _):
        lhs = []
        for o in range(8):
            pairs = []
            for q in range(0, 8, 2):
                k0 = jnp.minimum(step * 8 + q, K - 1)
                k1 = jnp.minimum(step * 8 + q + 1, K - 1)
                pairs.append(jnp.where(lower, cube[cls[k0, o]], cube[cls[k1, o]]))
            lhs.append(jnp.concatenate(pairs, axis=1))
        at = pl.multiple_of(step * 512, 512)
        acc[...] += dot(jnp.concatenate(lhs, axis=0), gath[pl.ds(at, 512), :])
        return 0

    lax.fori_loop(0, CHUNKS // 2, translate, 0)
    near = jnp.zeros((R, BOX), F32)
    for o in range(8):
        near = jnp.where(octant == o, acc[R * o:R * o + R, :], near)
    out_ref[...] = near + lifted

    for distance in DISTANCES:
        @pl.when(valid(distance))
        def _():
            rim_copy(distance).wait_send()


def shards(multipoles, partners, partner_offset, classes, m2l_ops, m2m_ops, coarse_ops, coupling, l2l_ops):
    any_space = pl.BlockSpec(memory_space=pl.ANY)
    vmem = pl.BlockSpec(memory_space=pltpu.VMEM)
    dma = pltpu.SemaphoreType.DMA
    return pl.pallas_call(
        kernel,
        name="far_field",
        out_shape=(
            jax.ShapeDtypeStruct((R, BOX), F32),
            jax.ShapeDtypeStruct((R, PARENTS), F32),
        ),
        in_specs=[any_space] * 9,
        out_specs=(vmem, vmem),
        scratch_shapes=[
            pltpu.VMEM((R, BOX), BF16),
            pltpu.VMEM((K, BOX), I32),
            pltpu.VMEM((K, BOX), I32),
            pltpu.SMEM((K, 128), I32),
            pltpu.VMEM((R, CLASSES * R), BF16),
            pltpu.VMEM((R, 8 * R), BF16),
            pltpu.VMEM((R, R), F32),
            pltpu.VMEM((COARSE, COARSE), F32),
            pltpu.VMEM((R, 8 * R), F32),
            pltpu.VMEM((R, 128), BF16),
            pltpu.VMEM((BLOCKS, R, 128), BF16),
            pltpu.VMEM((1, 128), F32),
            pltpu.VMEM((1, 128), F32),
            pltpu.VMEM((COARSE, 1, 128), F32),
            pltpu.VMEM((PAD_K, BOX), F32),
            pltpu.VMEM((PAD_K, BOX), I32),
            pltpu.VMEM((BLOCKS, R, 128), BF16),
            pltpu.VMEM((GROUPS * R, 256), BF16),
            pltpu.VMEM((CLASSES, R, 128), BF16),
            pltpu.VMEM((PAD_K * 64, BOX), BF16),
            pltpu.VMEM((8 * R, BOX), F32),
            dma((9,)),
            dma((BLOCKS,)),
            dma((BLOCKS,)),
            dma,
            dma,
            dma((3, 3)),
            dma((3, 3)),
        ],
        compiler_params=pltpu.CompilerParams(
            collective_id=0, has_side_effects=True, vmem_limit_bytes=48 * 1024 * 1024
        ),
    )(multipoles, partners, partner_offset, classes, m2l_ops, m2m_ops, coarse_ops, coupling, l2l_ops)


def solution(mesh):
    placed = (
        P(None, "box"), P(None, "box"), P(None, "box"), P(None, "box"),
        P(), P(), P(), P(), P(),
    )
    return jax.shard_map(
        shards,
        mesh=mesh,
        in_specs=placed,
        out_specs=(P(None, "box"), P(None, "box")),
        check_vma=False,
    )
```

time: 441 us -> 49.2 us (0.11); the launches traced: 433 us -> 48.4 us
  local copies, waits for them, and re-layouts: 173 us -> 9.4 us
  matrix products: 127 us -> 0 us
  blocking collectives: 64.6 us -> 0 us
  starting transfers between devices: 48.4 us -> 0 us
  Pallas kernels: 0 us -> 38.3 us
  other arithmetic: 15.3 us -> 0 us
    dot_general x36 -> x0, matrix products: 127 us -> none  [the longest x8 104 us: octant_terms(): jnp.dot(table, selector, preferred_element_type=jnp.float32)]
    psum x1 -> x0, blocking collectives: 64.6 us -> none  [shards(): coarse = lax.psum(share, 'box')]
    reshape x20 -> x0, local copies, waits for them, and re-layouts: 62.7 us -> none  [the longest x8 31.7 us: octant_terms(): stacked = gathered.reshape(rank * slots, count)]
    ppermute x14 -> x0, starting transfers between devices: 48.4 us -> none  [passed_along(): return lax.ppermute(x, axis, pairs)]
    pallas_call x0 -> x1, Pallas kernels: none -> 38.3 us  [shards(): pl.pallas_call(kernel, name='far_field', out_shape=(jax.ShapeDtypeStruct(...]
    gather x8 -> x0, local copies, waits for them, and re-layouts: 34.3 us -> none  [octant_terms(): picked = jnp.take(cube, classes_row, axis=1)]
    transpose x10 -> x0, local copies, waits for them, and re-layouts: 27.7 us -> none  [the longest x8 27.5 us: octant_terms(): operator = jnp.transpose(picked, (0, 2, 1)).reshape(rank, rank * slots)]
    slice x10 -> x0, local copies, waits for them, and re-layouts: 18.7 us -> none  [the longest x9 17.8 us: shards(): near = octant_terms(table, columns[:, octant::8], classes[:, octant], cube)]
  transfers between devices with their start and end apart: 14 -> 0, of which waited for: 2 -> 0; matrix products, arithmetic and copies ran while one was open for 36% -> 0% of each run, Pallas kernels for 0% -> 0%
where the time goes in v1:
time: 49.2 us; the launch traced here: 48.4 us
  Pallas kernels  38.3 us (78%)
  local copies, waits for them, and re-layouts  9.4 us (19%)
  between operations  0.66 us (1%)
    pallas_call x1, Pallas kernels, shards(): pl.pallas_call(kernel, name='far_field', out_shape=(jax.ShapeDtypeStruct(...  38.3 us
    unnamed x20, local copies, waits for them, and re-layouts  9.4 us

profile of v1, /device:TPU:3, one launch (start us, length us, event | category | flops | bytes accessed | tf_op | source)
XLA Modules:
  0.0 48.4 jit_solution(1329075276542012848)
XLA Ops:
  0.6 0.0 copy-start
  0.6 1.4 %copy-done = bf16[48,15168]{1,0:T(8,128)(2,1)S(1)} copy-done((bf16[48,15168]{1,0:T(8,128)(2,1)S(1)}, bf16[48,15168]{1,0:T(8,128)(2,1)}, u32[]{:S(2)}) %copy-start) | copy-done | bytes 1456152
  2.0 0.0 copy-start.1
  2.0 1.0 %copy-done.1 = s32[189,384]{1,0:T(8,128)S(1)} copy-done((s32[189,384]{1,0:T(8,128)S(1)}, s32[189,384]{1,0:T(8,128)}, u32[]{:S(2)}) %copy-start.1) | copy-done | bytes 290328
  3.0 0.0 copy-start.2
  3.0 1.0 %copy-done.2 = s32[189,384]{1,0:T(8,128)S(1)} copy-done((s32[189,384]{1,0:T(8,128)S(1)}, s32[189,384]{1,0:T(8,128)}, u32[]{:S(2)}) %copy-start.2) | copy-done | bytes 290328
  3.9 0.0 copy-start.3
  3.9 1.0 %copy-done.3 = s32[189,384]{1,0:T(8,128)S(1)} copy-done((s32[189,384]{1,0:T(8,128)S(1)}, s32[189,384]{1,0:T(8,128)}, u32[]{:S(2)}) %copy-start.3) | copy-done | bytes 290328
  4.9 0.0 copy-start.4
  4.9 0.9 %copy-done.4 = f32[48,384]{1,0:T(8,128)S(1)} copy-done((f32[48,384]{1,0:T(8,128)S(1)}, f32[48,384]{1,0:T(8,128)}, u32[]{:S(2)}) %copy-start.4) | copy-done | bytes 73752
  5.8 0.0 copy-start.5
  5.8 0.8 %copy-done.5 = bf16[48,384]{1,0:T(8,128)(2,1)S(1)} copy-done((bf16[48,384]{1,0:T(8,128)(2,1)S(1)}, bf16[48,384]{1,0:T(8,128)(2,1)}, u32[]{:S(2)}) %copy-start.5) | copy-done | bytes 36888
  6.5 0.0 copy-start.6
  6.5 0.8 %copy-done.6 = bf16[48,384]{1,0:T(8,128)(2,1)S(1)} copy-done((bf16[48,384]{1,0:T(8,128)(2,1)S(1)}, bf16[48,384]{1,0:T(8,128)(2,1)}, u32[]{:S(2)}) %copy-start.6) | copy-done | bytes 36888
  7.3 0.0 copy-start.7
  7.3 0.8 %copy-done.7 = f32[64,64]{1,0:T(8,128)S(1)} copy-done((f32[64,64]{1,0:T(8,128)S(1)}, f32[64,64]{1,0:T(8,128)}, u32[]{:S(2)}) %copy-start.7) | copy-done | bytes 16408
  8.1 0.0 copy-start.8
  8.1 0.7 %copy-done.8 = f32[48,48]{1,0:T(8,128)S(1)} copy-done((f32[48,48]{1,0:T(8,128)S(1)}, f32[48,48]{1,0:T(8,128)}, u32[]{:S(2)}) %copy-start.8) | copy-done | bytes 9240
  8.8 38.3 %far_field.1 = (f32[48,384]{1,0:T(8,128)S(1)}, f32[48,48]{1,0:T(8,128)S(1)}) custom-call(bf16[48,384]{1,0:T(8,128)(2,1)S(1)} %copy-done.5, s32[189,384]{1,0:T(8,128)S(1)} %copy-done.1, s32[189,384]{1,0:T(8,128)S(1)} %copy-done.2, s32[189,384]{1,0:T(8,128)S(1)} %copy-done.3, bf16[48,15168]{1,0:T(8,128)(2,1)S(1)} %copy-done, bf16[48,384]{1,0:T(8,128)(2,1)S(1)} %copy-done.6, ...), custom_call_target="tpu_custom_call" | custom-call | tf_op jit(solution)/shard_map/far_field/pallas_call | solution.py:334
  47.1 0.6 %copy.13 = f32[48,384]{1,0:T(8,128)} copy(f32[48,384]{1,0:T(8,128)S(1)} %get-tuple-element.4) | data formatting | bytes 147456
  47.7 0.6 %copy.14 = f32[48,48]{1,0:T(8,128)} copy(f32[48,48]{1,0:T(8,128)S(1)} %get-tuple-element.5) | data formatting | bytes 18432
Async XLA Ops:
  0.6 1.4 %copy-start = (bf16[48,15168]{1,0:T(8,128)(2,1)S(1)}, bf16[48,15168]{1,0:T(8,128)(2,1)}, u32[]{:S(2)}) copy-start(bf16[48,15168]{1,0:T(8,128)(2,1)} %m2l_hbm.1) | copy-start | bytes 4368388
  2.0 1.0 %copy-start.1 = (s32[189,384]{1,0:T(8,128)S(1)}, s32[189,384]{1,0:T(8,128)}, u32[]{:S(2)}) copy-start(s32[189,384]{1,0:T(8,128)} %part_hbm.1) | copy-start | bytes 870916
  3.0 1.0 %copy-start.2 = (s32[189,384]{1,0:T(8,128)S(1)}, s32[189,384]{1,0:T(8,128)}, u32[]{:S(2)}) copy-start(s32[189,384]{1,0:T(8,128)} %off_hbm.1) | copy-start | bytes 870916
  3.9 1.0 %copy-start.3 = (s32[189,384]{1,0:T(8,128)S(1)}, s32[189,384]{1,0:T(8,128)}, u32[]{:S(2)}) copy-start(s32[189,384]{1,0:T(8,128)} %cls_hbm.1) | copy-start | bytes 870916
  4.9 0.9 %copy-start.4 = (f32[48,384]{1,0:T(8,128)S(1)}, f32[48,384]{1,0:T(8,128)}, u32[]{:S(2)}) copy-start(f32[48,384]{1,0:T(8,128)} %l2l_hbm.1) | copy-start | bytes 221188
  5.8 0.8 %copy-start.5 = (bf16[48,384]{1,0:T(8,128)(2,1)S(1)}, bf16[48,384]{1,0:T(8,128)(2,1)}, u32[]{:S(2)}) copy-start(bf16[48,384]{1,0:T(8,128)(2,1)} %mult_hbm.1) | copy-start | bytes 110596
  6.5 0.8 %copy-start.6 = (bf16[48,384]{1,0:T(8,128)(2,1)S(1)}, bf16[48,384]{1,0:T(8,128)(2,1)}, u32[]{:S(2)}) copy-start(bf16[48,384]{1,0:T(8,128)(2,1)} %m2m_hbm.1) | copy-start | bytes 110596
  7.3 0.8 %copy-start.7 = (f32[64,64]{1,0:T(8,128)S(1)}, f32[64,64]{1,0:T(8,128)}, u32[]{:S(2)}) copy-start(f32[64,64]{1,0:T(8,128)} %coup_hbm.1) | copy-start | bytes 49156
  8.1 0.7 %copy-start.8 = (f32[48,48]{1,0:T(8,128)S(1)}, f32[48,48]{1,0:T(8,128)}, u32[]{:S(2)}) copy-start(f32[48,48]{1,0:T(8,128)} %cops_hbm.1) | copy-start | bytes 27652

commit v2 on v1

--- a/solution.py
+++ b/solution.py
@@ -25,9 +25,14 @@
 GROUP = 96
 BLOCKS = 2 * REACH
 GROUPS = BLOCKS // 2
-PAD_K = 192
-CHUNKS = PAD_K // 4
-FAR_ROWS = 64
+PAD_K = 190
+CHUNKS = PAD_K // 5
+STEPS = CHUNKS // 2
+LANE_SLOTS = (4, 9)
+PRODUCT_SLOTS = ((0, 1), (2, 3), (5, 6), (7, 8))
+PLACES = (
+    ((0, 0, 48),), ((48, 0, 48),), ((96, 0, 32), (240, 32, 16)), ((128, 0, 48),), ((176, 0, 48),),
+)
 
 
 def slot_of(distance):
@@ -51,11 +56,26 @@
     return lax.broadcasted_iota(I32, shape, dim)
 
 
+def lanes_from(x, source):
+    tiles = []
+    for v in range(3):
+        wanted = source[:, 128 * v:128 * v + 128]
+        inside, tile = wanted & 127, wanted >> 7
+        found = None
+        for u in range(3):
+            moved = jnp.take_along_axis(
+                x[:, 128 * u:128 * u + 128], inside, axis=1, mode="promise_in_bounds"
+            )
+            found = moved if u == 0 else jnp.where(tile == u, moved, found)
+        tiles.append(found)
+    return jnp.concatenate(tiles, axis=1)
+
+
 def kernel(
     mult_hbm, part_hbm, off_hbm, cls_hbm, m2l_hbm, m2m_hbm, cops_hbm, coup_hbm, l2l_hbm,
     out_ref, par_ref,
     mult, part, off, cls, m2l, m2m, cops, coup, l2l,
-    blk, rims, share, share_in, cbuf, lo_ref, hi_ref, strips, table, cube, gath, acc,
+    blk, rims, share, share_in, cbuf, cols, cols_ref, lo_ref, hi_ref, strips, table, wide, cube, gath, acc_a, acc_b,
     in_sem, rim_send, rim_recv, pair_send, pair_recv, far_send, far_recv,
 ):
     me = lax.axis_index("box")
@@ -105,6 +125,35 @@
     blk[...] = jnp.where(
         lane < RIM, own32[:, 0:128], jnp.where(lane < 2 * RIM, upper, 0.0)
     ).astype(BF16)
+
+    for i in range(BLOCKS):
+        if i < BOX // 32:
+            piece = own32[:, 128 * (i // 4):128 * (i // 4) + 128]
+            shift = (96 - 32 * (i % 4)) % 128
+            if shift:
+                piece = pltpu.roll(piece, shift, 1)
+            strips[i] = jnp.where(lane >= 2 * RIM, piece, 0.0).astype(BF16)
+        else:
+            strips[i] = jnp.zeros((R, 128), BF16)
+
+    loads[2].wait()
+    loads[3].wait()
+    within, half = part[...], off[...]
+    second = half & 1
+    pos = half >> 1
+    here = pos == REACH
+    local = within + 192 * second
+    local_col = ((local >> 5) << 7) + 96 + (local & 31)
+    block = jnp.where(pos > REACH, pos - 1, pos)
+    remote_col = (block << 7) + within + second * (RIM - 144)
+    col = jnp.where(here, local_col, remote_col)
+    cols[...] = jnp.full((192, BOX), 256 * GROUPS, I32)
+    cols[0:K, :] = col
+    slot = iota((192, BOX), 1)
+    col = lanes_from(cols[...], 8 * (slot % PARENTS) + slot // PARENTS)
+    cols_ref[...] = col
+    lo_ref[...] = (col & 255).astype(F32)
+    hi_ref[...] = col >> 8
 
     expected = jnp.minimum(me, REACH) + jnp.minimum(DEVICES - 1 - me, REACH) + 6
     pl.semaphore_wait(barrier, expected)
@@ -149,39 +198,11 @@
     )
     pair.start()
 
-    for i in range(BLOCKS):
-        if i < BOX // 32:
-            piece = own32[:, 128 * (i // 4):128 * (i // 4) + 128]
-            shift = (96 - 32 * (i % 4)) % 128
-            if shift:
-                piece = pltpu.roll(piece, shift, 1)
-            strips[i] = jnp.where(lane >= 2 * RIM, piece, 0.0).astype(BF16)
-        else:
-            strips[i] = jnp.zeros((R, 128), BF16)
-
-    loads[2].wait()
-    loads[3].wait()
-    lo_ref[...] = jnp.zeros((PAD_K, BOX), F32)
-    hi_ref[...] = jnp.full((PAD_K, BOX), GROUPS, I32)
-    within, half = part[...], off[...]
-    second = half & 1
-    pos = half >> 1
-    here = pos == REACH
-    local = within + 192 * second
-    local_col = ((local >> 5) << 7) + 96 + (local & 31)
-    block = jnp.where(pos > REACH, pos - 1, pos)
-    remote_col = (block << 7) + within + second * (RIM - 144)
-    col = jnp.where(here, local_col, remote_col)
-    lo_ref[0:K, :] = (col & 255).astype(F32)
-    hi_ref[0:K, :] = col >> 8
-
     loads[4].wait()
     row, column = iota((256, 512), 0), iota((256, 512), 1)
-    inner = column & 63
-    start = R * (column >> 7)
-    live = inner < R
-    first = jnp.where(live & (row == start + inner), 1.0, 0.0).astype(BF16)
-    second_half = jnp.where(live & (row == start + 64 + inner), 1.0, 0.0).astype(BF16)
+    wanted = R * (column >> 7) + (column & 127) % R
+    first = jnp.where(row == wanted, 1.0, 0.0).astype(BF16)
+    second_half = jnp.where(row == wanted + 64, 1.0, 0.0).astype(BF16)
 
     def spread(step, _):
         tops, bottoms = [], []
@@ -203,12 +224,12 @@
         cube[312 + j] = tail[:, 128 * j:128 * j + 128]
 
     def clear(step, _):
-        for q in range(4):
-            at = pl.multiple_of(step * 256 + 64 * q + R, 16)
-            gath[pl.ds(at, 16), :] = jnp.zeros((16, BOX), BF16)
+        at = pl.multiple_of(step * 256 + 224, 16)
+        gath[pl.ds(at, 16), :] = jnp.zeros((16, BOX), BF16)
         return 0
 
-    lax.fori_loop(0, CHUNKS, clear, 0)
+    lax.fori_loop(2, CHUNKS + 2, clear, 0)
+    gath[0:512, :] = jnp.zeros((512, BOX), BF16)
 
     pair.wait()
     cbuf[chip] = share[...] + share_in[...]
@@ -238,9 +259,9 @@
             rim_copy(-distance).wait_recv()
     for i in range(BLOCKS):
         g, side = i // 2, i % 2
-        table[R * g:R * g + R, 128 * side:128 * side + 128] = jnp.where(
-            lane < 2 * RIM, rims[i].astype(F32), strips[i].astype(F32)
-        ).astype(BF16)
+        columns = jnp.where(lane < 2 * RIM, rims[i].astype(F32), strips[i].astype(F32))
+        wide[i] = columns
+        table[R * g:R * g + R, 128 * side:128 * side + 128] = columns.astype(BF16)
 
     index = iota((256, 128), 0).astype(F32).astype(BF16)
 
@@ -253,34 +274,80 @@
             )
         return jnp.concatenate(pieces, axis=1)
 
-    def gather(step, _):
-        base = pl.multiple_of(step * 16, 16)
-        lo = lo_ref[pl.ds(base, 16), :]
-        hi = hi_ref[pl.ds(base, 16), :]
-        for p in range(0, 16, 2):
-            hot = jnp.concatenate([one_hot(lo, p), one_hot(lo, p + 1)], axis=1)
+    def keep(step, p, value):
+        for to, start, count in PLACES[p % 5]:
+            at = pl.multiple_of(step * 512 + 512 + 256 * (p // 5) + to, 16)
+            gath[pl.ds(at, count), :] = value[start:start + count]
+
+    def gather(step):
+        for p in LANE_SLOTS:
+            tiles = []
+            sought = cols_ref[pl.ds(step * 10 + p, 1), :]
+            for v in range(3):
+                wanted = jnp.broadcast_to(sought[:, 128 * v:128 * v + 128], (R, 128))
+                inside, tile = wanted & 127, wanted >> 7
+                value = jnp.zeros((R, 128), F32)
+                for i in range(BLOCKS):
+                    moved = jnp.take_along_axis(wide[i], inside, axis=1, mode="promise_in_bounds")
+                    value = jnp.where(tile == i, moved, value)
+                tiles.append(value.astype(BF16))
+            keep(step, p, jnp.concatenate(tiles, axis=1))
+        for pair_of in PRODUCT_SLOTS:
+            lo = [lo_ref[pl.ds(step * 10 + p, 1), :] for p in pair_of]
+            hi = [hi_ref[pl.ds(step * 10 + p, 1), :] for p in pair_of]
+            hot = jnp.concatenate([one_hot(x, 0) for x in lo], axis=1)
             found = dot(table[...], hot)
-            for q in range(2):
-                wanted = jnp.broadcast_to(hi[p + q:p + q + 1, :], (R, BOX))
+            for q, p in enumerate(pair_of):
+                wanted = jnp.broadcast_to(hi[q], (R, BOX))
                 value = jnp.zeros((R, BOX), F32)
                 for g in range(GROUPS):
                     part_of = found[R * g:R * g + R, BOX * q:BOX * q + BOX]
                     value = jnp.where(wanted == g, part_of, value)
-                at = pl.multiple_of(step * 1024 + 64 * (p + q), 64)
-                gath[pl.ds(at, R), :] = value.astype(BF16)
+                keep(step, p, value.astype(BF16))
+
+    loads[5].wait()
+    acc_a[...] = jnp.zeros(acc_a.shape, F32)
+    acc_b[...] = jnp.zeros(acc_b.shape, F32)
+    at_lane = iota((R, 128), 1).astype(F32).astype(BF16)
+    below_48 = at_lane < jnp.full((), 48, BF16)
+    below_96 = at_lane < jnp.full((), 96, BF16)
+
+    def translate(step, last):
+        first_slot = 10 * jnp.maximum(step - 1, 0)
+        lhs = []
+        for o in range(8):
+            tiles = []
+            for chunk in range(2):
+                ops = []
+                for q in range(5):
+                    k = first_slot + 5 * chunk + q
+                    if last and chunk and q == 4:
+                        k = jnp.minimum(k, K - 1)
+                    ops.append(cube[cls[k, o]])
+                tiles.append(jnp.where(below_48, ops[0], jnp.where(below_96, ops[1], ops[2])))
+                rest = pltpu.roll(ops[2], 32, 1)
+                tiles.append(jnp.where(below_48, ops[3], jnp.where(below_96, ops[4], rest)))
+            lhs.append(jnp.concatenate(tiles, axis=1))
+        at = pl.multiple_of(step * 512, 512)
+        acc_a[...] += dot(jnp.concatenate(lhs[0:6], axis=0), gath[pl.ds(at, 512), 0:256])
+        acc_b[...] += dot(jnp.concatenate(lhs[5:8], axis=0), gath[pl.ds(at, 512), 256:384])
+
+    def both(step, _):
+        translate(step, False)
+        gather(step)
         return 0
 
-    lax.fori_loop(0, 4, gather, 0)
+    lax.fori_loop(0, 6, both, 0)
     for copy in along_z:
         copy.wait()
     for copy in along_y:
         copy.start()
-    lax.fori_loop(4, 8, gather, 0)
+    lax.fori_loop(6, 12, both, 0)
     for copy in along_y:
         copy.wait()
     for copy in along_x:
         copy.start()
-    lax.fori_loop(8, 12, gather, 0)
+    lax.fori_loop(12, STEPS, both, 0)
     for copy in along_x:
         copy.wait()
 
@@ -295,31 +362,20 @@
     tile = (iota((R, BOX), 1) % R == iota((R, BOX), 0)).astype(F32)
     far_tiled = dot(far, tile, HIGHEST)
     terms = l2l[...] * far_tiled[0:1, :]
-    by_octant = (iota((BOX, BOX), 0) // R == iota((BOX, BOX), 1) % 8).astype(F32)
+    by_octant = (iota((BOX, BOX), 0) // R == iota((BOX, BOX), 1) // PARENTS).astype(F32)
     lifted = dot(terms, by_octant, HIGHEST)
 
-    loads[5].wait()
-    acc[...] = jnp.zeros(acc.shape, F32)
-    lower = iota((R, 128), 1).astype(F32).astype(BF16) < jnp.full((), 64, BF16)
-
-    def translate(step, _):
-        lhs = []
-        for o in range(8):
-            pairs = []
-            for q in range(0, 8, 2):
-                k0 = jnp.minimum(step * 8 + q, K - 1)
-                k1 = jnp.minimum(step * 8 + q + 1, K - 1)
-                pairs.append(jnp.where(lower, cube[cls[k0, o]], cube[cls[k1, o]]))
-            lhs.append(jnp.concatenate(pairs, axis=1))
-        at = pl.multiple_of(step * 512, 512)
-        acc[...] += dot(jnp.concatenate(lhs, axis=0), gath[pl.ds(at, 512), :])
-        return 0
-
-    lax.fori_loop(0, CHUNKS // 2, translate, 0)
-    near = jnp.zeros((R, BOX), F32)
-    for o in range(8):
-        near = jnp.where(octant == o, acc[R * o:R * o + R, :], near)
-    out_ref[...] = near + lifted
+    translate(STEPS, True)
+    left_octant = iota((R, 256), 1) // PARENTS
+    right_octant = (iota((R, 128), 1) + 256) // PARENTS
+    left, right = acc_a[0:R, :], acc_b[0:R, :]
+    for o in range(1, 6):
+        left = jnp.where(left_octant == o, acc_a[R * o:R * o + R, :], left)
+    for o in (6, 7):
+        right = jnp.where(right_octant == o, acc_b[R * (o - 5):R * (o - 5) + R, :], right)
+    sums = jnp.concatenate([left, right], axis=1) + lifted
+    box = iota((R, BOX), 1)
+    out_ref[...] = lanes_from(sums, PARENTS * (box % 8) + box // 8)
 
     for distance in DISTANCES:
         @pl.when(valid(distance))
@@ -355,13 +411,17 @@
             pltpu.VMEM((1, 128), F32),
             pltpu.VMEM((1, 128), F32),
             pltpu.VMEM((COARSE, 1, 128), F32),
-            pltpu.VMEM((PAD_K, BOX), F32),
-            pltpu.VMEM((PAD_K, BOX), I32),
+            pltpu.VMEM((192, BOX), I32),
+            pltpu.VMEM((192, BOX), I32),
+            pltpu.VMEM((192, BOX), F32),
+            pltpu.VMEM((192, BOX), I32),
             pltpu.VMEM((BLOCKS, R, 128), BF16),
             pltpu.VMEM((GROUPS * R, 256), BF16),
+            pltpu.VMEM((BLOCKS, R, 128), F32),
             pltpu.VMEM((CLASSES, R, 128), BF16),
-            pltpu.VMEM((PAD_K * 64, BOX), BF16),
-            pltpu.VMEM((8 * R, BOX), F32),
+            pltpu.VMEM(((CHUNKS + 2) * 256, BOX), BF16),
+            pltpu.VMEM((6 * R, 256), F32),
+            pltpu.VMEM((3 * R, 128), F32),
             dma((9,)),
             dma((BLOCKS,)),
             dma((BLOCKS,)),
@@ -371,7 +431,7 @@
             dma((3, 3)),
         ],
         compiler_params=pltpu.CompilerParams(
-            collective_id=0, has_side_effects=True, vmem_limit_bytes=48 * 1024 * 1024
+            collective_id=0, has_side_effects=True, vmem_limit_bytes=62 * 1024 * 1024
         ),
     )(multipoles, partners, partner_offset, classes, m2l_ops, m2m_ops, coarse_ops, coupling, l2l_ops)
 

time: 49.2 us -> 36.1 us (0.73)
  local copies, waits for them, and re-layouts: 9.4 us -> 2.87 us
  Pallas kernels: 38.3 us -> 32.2 us
    unnamed x20 -> x2, local copies, waits for them, and re-layouts: 9.4 us -> 2.87 us
    pallas_call x1, Pallas kernels: 38.3 us -> 32.2 us  [shards(): pl.pallas_call(kernel, name='far_field', out_shape=(jax.ShapeDtypeStruct(...]
where the time goes in v2:
time: 36.1 us; the launch traced here: 35.7 us
  Pallas kernels  32.2 us (89%)
  local copies, waits for them, and re-layouts  2.87 us (8%)
  between operations  0.64 us (2%)
    pallas_call x1, Pallas kernels, shards(): pl.pallas_call(kernel, name='far_field', out_shape=(jax.ShapeDtypeStruct(...  32.2 us
    unnamed x2, local copies, waits for them, and re-layouts  2.87 us

profile of v2, /device:TPU:3, one launch (start us, length us, event | category | flops | bytes accessed | tf_op | source)
XLA Modules:
  0.0 35.7 jit_solution(5616077450339596653)
XLA Ops:
  0.6 32.2 %far_field.1 = (f32[48,384]{1,0:T(8,128)}, f32[48,48]{1,0:T(8,128)}) custom-call(bf16[48,384]{1,0:T(8,128)(2,1)} %mult_hbm.1, s32[189,384]{1,0:T(8,128)} %part_hbm.1, s32[189,384]{1,0:T(8,128)} %off_hbm.1, s32[189,384]{1,0:T(8,128)} %cls_hbm.1, bf16[48,15168]{1,0:T(8,128)(2,1)} %m2l_hbm.1, bf16[48,384]{1,0:T(8,128)(2,1)} %m2m_hbm.1, f32[48,48]{1,0:T(8,128)} %cops_hbm.1, ...), custom_call_target="tpu_custom_call" | custom-call | tf_op jit(solution)/shard_map/far_field/pallas_call | solution.py:390
  32.9 1.5 %copy.13 = f32[48,384]{1,0:T(8,128)} copy(f32[48,384]{1,0:T(8,128)} %get-tuple-element.4) | data formatting | bytes 147456
  34.4 1.3 %copy.14 = f32[48,48]{1,0:T(8,128)} copy(f32[48,48]{1,0:T(8,128)} %get-tuple-element.5) | data formatting | bytes 18432

commit v3 on v2

--- a/solution.py
+++ b/solution.py
@@ -75,7 +75,7 @@
     mult_hbm, part_hbm, off_hbm, cls_hbm, m2l_hbm, m2m_hbm, cops_hbm, coup_hbm, l2l_hbm,
     out_ref, par_ref,
     mult, part, off, cls, m2l, m2m, cops, coup, l2l,
-    blk, rims, share, share_in, cbuf, cols, cols_ref, lo_ref, hi_ref, strips, table, wide, cube, gath, acc_a, acc_b,
+    blk, rims, share, share_in, cbuf, cols, cols_ref, lo_ref, hi_ref, strips, table, wide, cube, even, odd, acc_a, acc_b,
     in_sem, rim_send, rim_recv, pair_send, pair_recv, far_send, far_recv,
 ):
     me = lax.axis_index("box")
@@ -202,7 +202,7 @@
     row, column = iota((256, 512), 0), iota((256, 512), 1)
     wanted = R * (column >> 7) + (column & 127) % R
     first = jnp.where(row == wanted, 1.0, 0.0).astype(BF16)
-    second_half = jnp.where(row == wanted + 64, 1.0, 0.0).astype(BF16)
+    second_half = jnp.concatenate([jnp.zeros((64, 512), BF16), first[0:192]], axis=0)
 
     def spread(step, _):
         tops, bottoms = [], []
@@ -223,13 +223,8 @@
     for j in range(4):
         cube[312 + j] = tail[:, 128 * j:128 * j + 128]
 
-    def clear(step, _):
-        at = pl.multiple_of(step * 256 + 224, 16)
-        gath[pl.ds(at, 16), :] = jnp.zeros((16, BOX), BF16)
-        return 0
-
-    lax.fori_loop(2, CHUNKS + 2, clear, 0)
-    gath[0:512, :] = jnp.zeros((512, BOX), BF16)
+    for buffer in (even, odd):
+        buffer[...] = jnp.zeros((512, BOX), BF16)
 
     pair.wait()
     cbuf[chip] = share[...] + share_in[...]
@@ -274,36 +269,49 @@
             )
         return jnp.concatenate(pieces, axis=1)
 
-    def keep(step, p, value):
+    def keep(into, p, value):
         for to, start, count in PLACES[p % 5]:
-            at = pl.multiple_of(step * 512 + 512 + 256 * (p // 5) + to, 16)
-            gath[pl.ds(at, count), :] = value[start:start + count]
-
-    def gather(step):
-        for p in LANE_SLOTS:
-            tiles = []
-            sought = cols_ref[pl.ds(step * 10 + p, 1), :]
-            for v in range(3):
-                wanted = jnp.broadcast_to(sought[:, 128 * v:128 * v + 128], (R, 128))
-                inside, tile = wanted & 127, wanted >> 7
-                value = jnp.zeros((R, 128), F32)
-                for i in range(BLOCKS):
-                    moved = jnp.take_along_axis(wide[i], inside, axis=1, mode="promise_in_bounds")
-                    value = jnp.where(tile == i, moved, value)
-                tiles.append(value.astype(BF16))
-            keep(step, p, jnp.concatenate(tiles, axis=1))
-        for pair_of in PRODUCT_SLOTS:
-            lo = [lo_ref[pl.ds(step * 10 + p, 1), :] for p in pair_of]
-            hi = [hi_ref[pl.ds(step * 10 + p, 1), :] for p in pair_of]
-            hot = jnp.concatenate([one_hot(x, 0) for x in lo], axis=1)
-            found = dot(table[...], hot)
-            for q, p in enumerate(pair_of):
-                wanted = jnp.broadcast_to(hi[q], (R, BOX))
-                value = jnp.zeros((R, BOX), F32)
-                for g in range(GROUPS):
-                    part_of = found[R * g:R * g + R, BOX * q:BOX * q + BOX]
-                    value = jnp.where(wanted == g, part_of, value)
-                keep(step, p, value.astype(BF16))
+            at = 256 * (p // 5) + to
+            into[at:at + count, :] = value[start:start + count]
+
+    def by_lanes(into, p, sought, v):
+        wanted = jnp.broadcast_to(sought[:, 128 * v:128 * v + 128], (R, 128))
+        inside, tile = wanted & 127, wanted >> 7
+        value = jnp.zeros((R, 128), F32)
+        for i in range(BLOCKS):
+            moved = jnp.take_along_axis(wide[i], inside, axis=1, mode="promise_in_bounds")
+            value = jnp.where(tile == i, moved, value)
+        value = value.astype(BF16)
+        for to, start, count in PLACES[p % 5]:
+            at = 256 * (p // 5) + to
+            into[at:at + count, 128 * v:128 * v + 128] = value[start:start + count]
+
+    def by_product(step, into, pair_of):
+        lo = [lo_ref[pl.ds(step * 10 + p, 1), :] for p in pair_of]
+        hi = [hi_ref[pl.ds(step * 10 + p, 1), :] for p in pair_of]
+        hot = jnp.concatenate([one_hot(x, 0) for x in lo], axis=1)
+        found = dot(table[...], hot)
+        for q, p in enumerate(pair_of):
+            wanted = jnp.broadcast_to(hi[q], (R, BOX))
+            value = jnp.zeros((R, BOX), F32)
+            for g in range(GROUPS):
+                part_of = found[R * g:R * g + R, BOX * q:BOX * q + BOX]
+                value = jnp.where(wanted == g, part_of, value)
+            keep(into, p, value.astype(BF16))
+
+    def gather(step, into, other):
+        sought = {p: cols_ref[pl.ds(step * 10 + p, 1), :] for p in LANE_SLOTS}
+        by_product(step, into, PRODUCT_SLOTS[0])
+        by_lanes(into, LANE_SLOTS[0], sought[LANE_SLOTS[0]], 0)
+        by_lanes(into, LANE_SLOTS[0], sought[LANE_SLOTS[0]], 1)
+        by_product(step, into, PRODUCT_SLOTS[1])
+        by_lanes(into, LANE_SLOTS[0], sought[LANE_SLOTS[0]], 2)
+        translate(step, other, False)
+        by_lanes(into, LANE_SLOTS[1], sought[LANE_SLOTS[1]], 0)
+        by_product(step, into, PRODUCT_SLOTS[2])
+        by_lanes(into, LANE_SLOTS[1], sought[LANE_SLOTS[1]], 1)
+        by_lanes(into, LANE_SLOTS[1], sought[LANE_SLOTS[1]], 2)
+        by_product(step, into, PRODUCT_SLOTS[3])
 
     loads[5].wait()
     acc_a[...] = jnp.zeros(acc_a.shape, F32)
@@ -312,7 +320,7 @@
     below_48 = at_lane < jnp.full((), 48, BF16)
     below_96 = at_lane < jnp.full((), 96, BF16)
 
-    def translate(step, last):
+    def translate(step, source, last):
         first_slot = 10 * jnp.maximum(step - 1, 0)
         lhs = []
         for o in range(8):
@@ -328,26 +336,25 @@
                 rest = pltpu.roll(ops[2], 32, 1)
                 tiles.append(jnp.where(below_48, ops[3], jnp.where(below_96, ops[4], rest)))
             lhs.append(jnp.concatenate(tiles, axis=1))
-        at = pl.multiple_of(step * 512, 512)
-        acc_a[...] += dot(jnp.concatenate(lhs[0:6], axis=0), gath[pl.ds(at, 512), 0:256])
-        acc_b[...] += dot(jnp.concatenate(lhs[5:8], axis=0), gath[pl.ds(at, 512), 256:384])
+        acc_a[...] += dot(jnp.concatenate(lhs[0:6], axis=0), source[:, 0:256])
+        acc_b[...] += dot(jnp.concatenate(lhs[5:8], axis=0), source[:, 256:384])
 
     def both(step, _):
-        translate(step, False)
-        gather(step)
+        gather(2 * step, even, odd)
+        gather(2 * step + 1, odd, even)
         return 0
 
-    lax.fori_loop(0, 6, both, 0)
+    lax.fori_loop(0, 3, both, 0)
     for copy in along_z:
         copy.wait()
     for copy in along_y:
         copy.start()
-    lax.fori_loop(6, 12, both, 0)
+    lax.fori_loop(3, 6, both, 0)
     for copy in along_y:
         copy.wait()
     for copy in along_x:
         copy.start()
-    lax.fori_loop(12, STEPS, both, 0)
+    lax.fori_loop(6, STEPS // 2, both, 0)
     for copy in along_x:
         copy.wait()
 
@@ -365,7 +372,8 @@
     by_octant = (iota((BOX, BOX), 0) // R == iota((BOX, BOX), 1) // PARENTS).astype(F32)
     lifted = dot(terms, by_octant, HIGHEST)
 
-    translate(STEPS, True)
+    gather(STEPS - 1, even, odd)
+    translate(STEPS, even, True)
     left_octant = iota((R, 256), 1) // PARENTS
     right_octant = (iota((R, 128), 1) + 256) // PARENTS
     left, right = acc_a[0:R, :], acc_b[0:R, :]
@@ -419,7 +427,8 @@
             pltpu.VMEM((GROUPS * R, 256), BF16),
             pltpu.VMEM((BLOCKS, R, 128), F32),
             pltpu.VMEM((CLASSES, R, 128), BF16),
-            pltpu.VMEM(((CHUNKS + 2) * 256, BOX), BF16),
+            pltpu.VMEM((512, BOX), BF16),
+            pltpu.VMEM((512, BOX), BF16),
             pltpu.VMEM((6 * R, 256), F32),
             pltpu.VMEM((3 * R, 128), F32),
             dma((9,)),
@@ -431,9 +440,15 @@
             dma((3, 3)),
         ],
         compiler_params=pltpu.CompilerParams(
-            collective_id=0, has_side_effects=True, vmem_limit_bytes=62 * 1024 * 1024
+            collective_id=0, has_side_effects=True, vmem_limit_bytes=40 * 1024 * 1024
         ),
-    )(multipoles, partners, partner_offset, classes, m2l_ops, m2m_ops, coarse_ops, coupling, l2l_ops)
+    )(*[
+        pltpu.with_memory_space_constraint(x, pltpu.HBM)
+        for x in (
+            multipoles, partners, partner_offset, classes, m2l_ops, m2m_ops, coarse_ops, coupling,
+            l2l_ops,
+        )
+    ])
 
 
 def solution(mesh):

time: 36.1 us -> 30.6 us (0.85)
  Pallas kernels: 32.2 us -> 28.6 us
  local copies, waits for them, and re-layouts: 2.87 us -> 1.24 us
    pallas_call x1, Pallas kernels: 32.2 us -> 28.6 us  [shards(): pl.pallas_call(kernel, name='far_field', out_shape=(jax.ShapeDtypeStruct(...]
    unnamed x2, local copies, waits for them, and re-layouts: 2.87 us -> 1.24 us
where the time goes in v3:
time: 30.6 us; the launch traced here: 30.5 us
  Pallas kernels  28.6 us (93%)
  local copies, waits for them, and re-layouts  1.24 us (4%)
  between operations  0.64 us (2%)
    pallas_call x1, Pallas kernels, shards(): pl.pallas_call(kernel, name='far_field', out_shape=(jax.ShapeDtypeStruct(...  28.6 us
    unnamed x2, local copies, waits for them, and re-layouts  1.24 us

profile of v3, /device:TPU:3, one launch (start us, length us, event | category | flops | bytes accessed | tf_op | source)
XLA Modules:
  0.0 30.5 jit_solution(16595665947632011556)
XLA Ops:
  0.6 28.6 %far_field.1 = (f32[48,384]{1,0:T(8,128)S(1)}, f32[48,48]{1,0:T(8,128)S(1)}) custom-call(bf16[48,384]{1,0:T(8,128)(2,1)} %mult_hbm.1, s32[189,384]{1,0:T(8,128)} %part_hbm.1, s32[189,384]{1,0:T(8,128)} %off_hbm.1, s32[189,384]{1,0:T(8,128)} %cls_hbm.1, bf16[48,15168]{1,0:T(8,128)(2,1)} %m2l_hbm.1, bf16[48,384]{1,0:T(8,128)(2,1)} %m2m_hbm.1, ...), custom_call_target="tpu_custom_call" | custom-call | tf_op jit(solution)/shard_map/far_field/pallas_call | solution.py:398
  29.2 0.6 %copy.13 = f32[48,384]{1,0:T(8,128)} copy(f32[48,384]{1,0:T(8,128)S(1)} %get-tuple-element.4) | data formatting | bytes 147456
  29.9 0.6 %copy.14 = f32[48,48]{1,0:T(8,128)} copy(f32[48,48]{1,0:T(8,128)S(1)} %get-tuple-element.5) | data formatting | bytes 18432

commit v4 on v3

--- a/solution.py
+++ b/solution.py
@@ -147,7 +147,7 @@
     block = jnp.where(pos > REACH, pos - 1, pos)
     remote_col = (block << 7) + within + second * (RIM - 144)
     col = jnp.where(here, local_col, remote_col)
-    cols[...] = jnp.full((192, BOX), 256 * GROUPS, I32)
+    cols[...] = jnp.zeros((192, BOX), I32)
     cols[0:K, :] = col
     slot = iota((192, BOX), 1)
     col = lanes_from(cols[...], 8 * (slot % PARENTS) + slot // PARENTS)
@@ -206,19 +206,19 @@
 
     def spread(step, _):
         tops, bottoms = [], []
-        for u in range(3):
-            base = pl.multiple_of((step * 3 + u) * 384, 128)
+        for u in range(13):
+            base = pl.multiple_of((step * 13 + u) * 384, 128)
             tops.append(m2l[:, pl.ds(base, 256)])
             bottoms.append(m2l[:, pl.ds(pl.multiple_of(base + 128, 128), 256)])
         a = dot(jnp.concatenate(tops, axis=0), first).astype(BF16)
         b = dot(jnp.concatenate(bottoms, axis=0), second_half).astype(BF16)
-        for u in range(3):
+        for u in range(13):
             for j in range(4):
-                cube[(step * 3 + u) * 8 + j] = a[R * u:R * u + R, 128 * j:128 * j + 128]
-                cube[(step * 3 + u) * 8 + 4 + j] = b[R * u:R * u + R, 128 * j:128 * j + 128]
+                cube[(step * 13 + u) * 8 + j] = a[R * u:R * u + R, 128 * j:128 * j + 128]
+                cube[(step * 13 + u) * 8 + 4 + j] = b[R * u:R * u + R, 128 * j:128 * j + 128]
         return 0
 
-    lax.fori_loop(0, 13, spread, 0)
+    lax.fori_loop(0, 3, spread, 0)
     tail = dot(m2l[:, 39 * 384:CLASSES * R], first[0:192, :]).astype(BF16)
     for j in range(4):
         cube[312 + j] = tail[:, 128 * j:128 * j + 128]
@@ -277,10 +277,10 @@
     def by_lanes(into, p, sought, v):
         wanted = jnp.broadcast_to(sought[:, 128 * v:128 * v + 128], (R, 128))
         inside, tile = wanted & 127, wanted >> 7
-        value = jnp.zeros((R, 128), F32)
+        value = None
         for i in range(BLOCKS):
             moved = jnp.take_along_axis(wide[i], inside, axis=1, mode="promise_in_bounds")
-            value = jnp.where(tile == i, moved, value)
+            value = moved if i == 0 else jnp.where(tile == i, moved, value)
         value = value.astype(BF16)
         for to, start, count in PLACES[p % 5]:
             at = 256 * (p // 5) + to
@@ -293,8 +293,8 @@
         found = dot(table[...], hot)
         for q, p in enumerate(pair_of):
             wanted = jnp.broadcast_to(hi[q], (R, BOX))
-            value = jnp.zeros((R, BOX), F32)
-            for g in range(GROUPS):
+            value = found[0:R, BOX * q:BOX * q + BOX]
+            for g in range(1, GROUPS):
                 part_of = found[R * g:R * g + R, BOX * q:BOX * q + BOX]
                 value = jnp.where(wanted == g, part_of, value)
             keep(into, p, value.astype(BF16))
@@ -330,8 +330,9 @@
                 for q in range(5):
                     k = first_slot + 5 * chunk + q
                     if last and chunk and q == 4:
-                        k = jnp.minimum(k, K - 1)
-                    ops.append(cube[cls[k, o]])
+                        ops.append(jnp.zeros((R, 128), BF16))
+                    else:
+                        ops.append(cube[cls[k, o]])
                 tiles.append(jnp.where(below_48, ops[0], jnp.where(below_96, ops[1], ops[2])))
                 rest = pltpu.roll(ops[2], 32, 1)
                 tiles.append(jnp.where(below_48, ops[3], jnp.where(below_96, ops[4], rest)))
@@ -339,22 +340,30 @@
         acc_a[...] += dot(jnp.concatenate(lhs[0:6], axis=0), source[:, 0:256])
         acc_b[...] += dot(jnp.concatenate(lhs[5:8], axis=0), source[:, 256:384])
 
-    def both(step, _):
-        gather(2 * step, even, odd)
-        gather(2 * step + 1, odd, even)
+    def several(step, _):
+        @pl.when(step == 1)
+        def _():
+            for copy in along_z:
+                copy.wait()
+            for copy in along_y:
+                copy.start()
+
+        @pl.when(step == 2)
+        def _():
+            for copy in along_y:
+                copy.wait()
+            for copy in along_x:
+                copy.start()
+
+        gather(6 * step + 0, even, odd)
+        gather(6 * step + 1, odd, even)
+        gather(6 * step + 2, even, odd)
+        gather(6 * step + 3, odd, even)
+        gather(6 * step + 4, even, odd)
+        gather(6 * step + 5, odd, even)
         return 0
 
-    lax.fori_loop(0, 3, both, 0)
-    for copy in along_z:
-        copy.wait()
-    for copy in along_y:
-        copy.start()
-    lax.fori_loop(3, 6, both, 0)
-    for copy in along_y:
-        copy.wait()
-    for copy in along_x:
-        copy.start()
-    lax.fori_loop(6, STEPS // 2, both, 0)
+    lax.fori_loop(0, 3, several, 0)
     for copy in along_x:
         copy.wait()
 

time: 30.6 us -> 29.7 us (0.971)
  Pallas kernels: 28.6 us -> 27.7 us
    pallas_call x1, Pallas kernels: 28.6 us -> 27.7 us  [shards(): pl.pallas_call(kernel, name='far_field', out_shape=(jax.ShapeDtypeStruct(...]
where the time goes in v4:
time: 29.7 us; the launch traced here: 29.6 us
  Pallas kernels  27.7 us (93%)
  local copies, waits for them, and re-layouts  1.24 us (4%)
  between operations  0.64 us (2%)
    pallas_call x1, Pallas kernels, shards(): pl.pallas_call(kernel, name='far_field', out_shape=(jax.ShapeDtypeStruct(...  27.7 us
    unnamed x2, local copies, waits for them, and re-layouts  1.24 us

profile of v4, /device:TPU:3, one launch (start us, length us, event | category | flops | bytes accessed | tf_op | source)
XLA Modules:
  0.0 29.6 jit_solution(16106819362732671940)
XLA Ops:
  0.6 27.7 %far_field.1 = (f32[48,384]{1,0:T(8,128)S(1)}, f32[48,48]{1,0:T(8,128)S(1)}) custom-call(bf16[48,384]{1,0:T(8,128)(2,1)} %mult_hbm.1, s32[189,384]{1,0:T(8,128)} %part_hbm.1, s32[189,384]{1,0:T(8,128)} %off_hbm.1, s32[189,384]{1,0:T(8,128)} %cls_hbm.1, bf16[48,15168]{1,0:T(8,128)(2,1)} %m2l_hbm.1, bf16[48,384]{1,0:T(8,128)(2,1)} %m2m_hbm.1, ...), custom_call_target="tpu_custom_call" | custom-call | tf_op jit(solution)/shard_map/far_field/pallas_call | solution.py:407
  28.3 0.6 %copy.13 = f32[48,384]{1,0:T(8,128)} copy(f32[48,384]{1,0:T(8,128)S(1)} %get-tuple-element.4) | data formatting | bytes 147456
  29.0 0.6 %copy.14 = f32[48,48]{1,0:T(8,128)} copy(f32[48,48]{1,0:T(8,128)S(1)} %get-tuple-element.5) | data formatting | bytes 18432

commit v5 on v4

--- a/solution.py
+++ b/solution.py
@@ -337,12 +337,16 @@
                 rest = pltpu.roll(ops[2], 32, 1)
                 tiles.append(jnp.where(below_48, ops[3], jnp.where(below_96, ops[4], rest)))
             lhs.append(jnp.concatenate(tiles, axis=1))
-        acc_a[...] += dot(jnp.concatenate(lhs[0:6], axis=0), source[:, 0:256])
-        acc_b[...] += dot(jnp.concatenate(lhs[5:8], axis=0), source[:, 256:384])
+        acc_a[...] += dot(jnp.concatenate(lhs[0:5], axis=0), source[:, 0:256])
+        acc_b[...] += dot(jnp.concatenate(lhs[5:8], axis=0), source[:, 128:384])
 
     def several(step, _):
         @pl.when(step == 1)
         def _():
+            for distance in DISTANCES:
+                @pl.when(valid(distance))
+                def _():
+                    rim_copy(distance).wait_send()
             for copy in along_z:
                 copy.wait()
             for copy in along_y:
@@ -383,21 +387,18 @@
 
     gather(STEPS - 1, even, odd)
     translate(STEPS, even, True)
-    left_octant = iota((R, 256), 1) // PARENTS
-    right_octant = (iota((R, 128), 1) + 256) // PARENTS
-    left, right = acc_a[0:R, :], acc_b[0:R, :]
-    for o in range(1, 6):
-        left = jnp.where(left_octant == o, acc_a[R * o:R * o + R, :], left)
-    for o in (6, 7):
-        right = jnp.where(right_octant == o, acc_b[R * (o - 5):R * (o - 5) + R, :], right)
-    sums = jnp.concatenate([left, right], axis=1) + lifted
+    octant = iota((R, BOX), 1) // PARENTS
+    none = jnp.zeros((R, 128), F32)
+    sums = jnp.concatenate([acc_a[0:R, :], none], axis=1)
+    for o in range(1, 8):
+        if o < 5:
+            rows = jnp.concatenate([acc_a[R * o:R * o + R, :], none], axis=1)
+        else:
+            rows = jnp.concatenate([none, acc_b[R * (o - 5):R * (o - 5) + R, :]], axis=1)
+        sums = jnp.where(octant == o, rows, sums)
+    sums = sums + lifted
     box = iota((R, BOX), 1)
     out_ref[...] = lanes_from(sums, PARENTS * (box % 8) + box // 8)
-
-    for distance in DISTANCES:
-        @pl.when(valid(distance))
-        def _():
-            rim_copy(distance).wait_send()
 
 
 def shards(multipoles, partners, partner_offset, classes, m2l_ops, m2m_ops, coarse_ops, coupling, l2l_ops):
@@ -438,8 +439,8 @@
             pltpu.VMEM((CLASSES, R, 128), BF16),
             pltpu.VMEM((512, BOX), BF16),
             pltpu.VMEM((512, BOX), BF16),
-            pltpu.VMEM((6 * R, 256), F32),
-            pltpu.VMEM((3 * R, 128), F32),
+            pltpu.VMEM((5 * R, 256), F32),
+            pltpu.VMEM((3 * R, 256), F32),
             dma((9,)),
             dma((BLOCKS,)),
             dma((BLOCKS,)),

time: 29.7 us -> 29.5 us (level)
  no operation moved by 1% of the time
where the time goes in v5:
time: 29.5 us; the launch traced here: 29.4 us
  Pallas kernels  27.5 us (93%)
  local copies, waits for them, and re-layouts  1.24 us (4%)
  between operations  0.64 us (2%)
    pallas_call x1, Pallas kernels, shards(): pl.pallas_call(kernel, name='far_field', out_shape=(jax.ShapeDtypeStruct(...  27.5 us
    unnamed x2, local copies, waits for them, and re-layouts  1.24 us

profile of v5, /device:TPU:3, one launch (start us, length us, event | category | flops | bytes accessed | tf_op | source)
XLA Modules:
  0.0 29.4 jit_solution(11358637605888595054)
XLA Ops:
  0.6 27.5 %far_field.1 = (f32[48,384]{1,0:T(8,128)S(1)}, f32[48,48]{1,0:T(8,128)S(1)}) custom-call(bf16[48,384]{1,0:T(8,128)(2,1)} %mult_hbm.1, s32[189,384]{1,0:T(8,128)} %part_hbm.1, s32[189,384]{1,0:T(8,128)} %off_hbm.1, s32[189,384]{1,0:T(8,128)} %cls_hbm.1, bf16[48,15168]{1,0:T(8,128)(2,1)} %m2l_hbm.1, bf16[48,384]{1,0:T(8,128)(2,1)} %m2m_hbm.1, ...), custom_call_target="tpu_custom_call" | custom-call | tf_op jit(solution)/shard_map/far_field/pallas_call | solution.py:408
  28.1 0.6 %copy.13 = f32[48,384]{1,0:T(8,128)} copy(f32[48,384]{1,0:T(8,128)S(1)} %get-tuple-element.4) | data formatting | bytes 147456
  28.8 0.6 %copy.14 = f32[48,48]{1,0:T(8,128)} copy(f32[48,48]{1,0:T(8,128)S(1)} %get-tuple-element.5) | data formatting | bytes 18432

commit v6 on v5

--- a/solution.py
+++ b/solution.py
@@ -252,7 +252,8 @@
         @pl.when(valid(distance))
         def _():
             rim_copy(-distance).wait_recv()
-    for i in range(BLOCKS):
+
+        i = slot_of(distance)
         g, side = i // 2, i % 2
         columns = jnp.where(lane < 2 * RIM, rims[i].astype(F32), strips[i].astype(F32))
         wide[i] = columns

time: 29.5 us -> 29.5 us (level)
  no operation moved by 1% of the time
where the time goes in v6:
time: 29.5 us; the launch traced here: 29.3 us
  Pallas kernels  27.5 us (93%)
  local copies, waits for them, and re-layouts  1.24 us (4%)
  between operations  0.64 us (2%)
    pallas_call x1, Pallas kernels, shards(): pl.pallas_call(kernel, name='far_field', out_shape=(jax.ShapeDtypeStruct(...  27.5 us
    unnamed x2, local copies, waits for them, and re-layouts  1.24 us

profile of v6, /device:TPU:3, one launch (start us, length us, event | category | flops | bytes accessed | tf_op | source)
XLA Modules:
  0.0 29.3 jit_solution(566109049971503541)
XLA Ops:
  0.6 27.5 %far_field.1 = (f32[48,384]{1,0:T(8,128)S(1)}, f32[48,48]{1,0:T(8,128)S(1)}) custom-call(bf16[48,384]{1,0:T(8,128)(2,1)} %mult_hbm.1, s32[189,384]{1,0:T(8,128)} %part_hbm.1, s32[189,384]{1,0:T(8,128)} %off_hbm.1, s32[189,384]{1,0:T(8,128)} %cls_hbm.1, bf16[48,15168]{1,0:T(8,128)(2,1)} %m2l_hbm.1, bf16[48,384]{1,0:T(8,128)(2,1)} %m2m_hbm.1, ...), custom_call_target="tpu_custom_call" | custom-call | tf_op jit(solution)/shard_map/far_field/pallas_call | solution.py:409
  28.1 0.6 %copy.13 = f32[48,384]{1,0:T(8,128)} copy(f32[48,384]{1,0:T(8,128)S(1)} %get-tuple-element.4) | data formatting | bytes 147456
  28.7 0.6 %copy.14 = f32[48,48]{1,0:T(8,128)} copy(f32[48,48]{1,0:T(8,128)S(1)} %get-tuple-element.5) | data formatting | bytes 18432
